TPU v7x, 32 devices: a whole 2x2x4 slice. The times are simulated.
32 devices in a mesh: dp: 2 (over x), fsdp: 16 (over z, y, core).
Axes of the slice: x: 2, y: 2, z: 4, core: 2. Of those that a mesh axis runs over, the one named last changes fastest.
Arguments:
- pixels: bfloat16 [23552, 512], P(('dp', 'fsdp')), may hold values from -6 to 6
- embedding: bfloat16 [96, 2048], P(('dp', 'fsdp')), may hold values from -6 to 6
- text_states: bfloat16 [96, 77, 4096], P(('dp', 'fsdp')), may hold values from -6 to 6
- text_mask: int32 [96, 77], P(('dp', 'fsdp')), may hold values 0 or 1
- occupancy: int32 [32, 3], P(('dp', 'fsdp')), may hold values 0 or 1
- cotangent: bfloat16 [23552, 1024], P(('dp', 'fsdp')), may hold values from -6 to 6
- in_gain: bfloat16 [512], P('fsdp'), may hold values from 0.5 to 1.5
- in_shift: bfloat16 [512], P('fsdp'), may hold values from -3 to 3
- conv_first: bfloat16 [4608, 1024], P('fsdp'), may hold values from -0.09375 to 0.09375
- first_bias: bfloat16 [1024], P('fsdp'), may hold values from -2 to 2
- emb_weight: bfloat16 [2048, 2048], P('fsdp'), may hold values from -0.0625 to 0.0625
- emb_bias: bfloat16 [2048], P('fsdp'), may hold values from -2 to 2
- mid_gain: bfloat16 [1024], P('fsdp'), may hold values from 0.5 to 1.5
- mid_shift: bfloat16 [1024], P('fsdp'), may hold values from -3 to 3
- conv_second: bfloat16 [9216, 1024], P('fsdp'), may hold values from -0.0625 to 0.0625
- second_bias: bfloat16 [1024], P('fsdp'), may hold values from -2 to 2
- skip_weight: bfloat16 [512, 1024], P('fsdp'), may hold values from -0.25 to 0.25
- skip_bias: bfloat16 [1024], P('fsdp'), may hold values from -2 to 2
- attn_gain: bfloat16 [1024], P('fsdp'), may hold values from 0.5 to 1.5
- attn_shift: bfloat16 [1024], P('fsdp'), may hold values from -3 to 3
- attend_weight: bfloat16 [1024, 1536], P('fsdp'), may hold values from -0.1875 to 0.1875
- text_weight: bfloat16 [4096, 1024], P('fsdp'), may hold values from -0.09375 to 0.09375
- out_weight: bfloat16 [512, 1024], P('fsdp'), may hold values from -1.5 to 1.5
- out_bias: bfloat16 [1024], P('fsdp'), may hold values from -2 to 2
Outputs:
- block_output: bfloat16 [23552, 1024], P(('dp', 'fsdp'))
- grad_pixels: float32 [23552, 512], P(('dp', 'fsdp'))
- grad_in_gain: float32 [512], P('fsdp')
- grad_in_shift: float32 [512], P('fsdp')
- grad_conv_first: float32 [4608, 1024], P('fsdp')
- grad_first_bias: float32 [1024], P('fsdp')
- grad_emb_weight: float32 [2048, 2048], P('fsdp')
- grad_emb_bias: float32 [2048], P('fsdp')
- grad_mid_gain: float32 [1024], P('fsdp')
- grad_mid_shift: float32 [1024], P('fsdp')
- grad_conv_second: float32 [9216, 1024], P('fsdp')
- grad_second_bias: float32 [1024], P('fsdp')
- grad_skip_weight: float32 [512, 1024], P('fsdp')
- grad_skip_bias: float32 [1024], P('fsdp')
- grad_attn_gain: float32 [1024], P('fsdp')
- grad_attn_shift: float32 [1024], P('fsdp')
- grad_attend_weight: float32 [1024, 1536], P('fsdp')
- grad_text_weight: float32 [4096, 1024], P('fsdp')
- grad_out_weight: float32 [512, 1024], P('fsdp')
- grad_out_bias: float32 [1024], P('fsdp')
All inputs are finite; a program needn't handle non-finite values. No bound on the sum of `text_mask` or of `occupancy` on one device may be relied on, other than what follows from the above.
Results may differ from a plain program's by a relative error of at most 0.02.
Values may be sent and summed in bfloat16 or wider, within the bound.
A program may use at most 320 MiB of HBM per device.

v0:
```python
import jax
import jax.numpy as jnp
from jax import lax
from jax.sharding import PartitionSpec as P

HEADS = 8
HEAD = 64
GROUPS = 32
UNIT = 4


def for_sending(array):

    def short(part):
        return part.astype(jnp.bfloat16) if part.dtype == jnp.float32 else part

    return jax.tree.map(short, array)


def product(first_operand, second_operand):
    return jnp.dot(first_operand, second_operand, preferred_element_type=jnp.float32)


def product_left(first_operand, second_operand):
    return lax.dot_general(
        first_operand, second_operand, (((0,), (0,)), ((), ())), preferred_element_type=jnp.float32
    )


def product_right(first_operand, second_operand):
    return lax.dot_general(
        first_operand, second_operand, (((1,), (1,)), ((), ())), preferred_element_type=jnp.float32
    )


def group_norm(entries, norm_gain, norm_shift):
    pixel_count, channels = entries.shape
    grouped = entries.reshape(pixel_count, GROUPS, channels // GROUPS)
    center = jnp.mean(grouped, axis=(0, 2), keepdims=True)
    spread = jnp.mean(jnp.square(grouped - center), axis=(0, 2), keepdims=True)
    scaled = ((grouped - center) * lax.rsqrt(spread + 1e-05)).reshape(pixel_count, channels)
    return scaled * norm_gain + norm_shift


def first_activation(pixel_float, norm_gain, norm_shift):
    return jax.nn.silu(group_norm(pixel_float, norm_gain, norm_shift))


def middle_activation(first_conv, scale_part, shift_part, norm_gain, norm_shift):
    return jax.nn.silu(
        group_norm(first_conv, norm_gain, norm_shift) * (1.0 + scale_part) + shift_part
    )


def patches(flat_rows, height, breadth):
    channels = flat_rows.shape[-1]
    picture = flat_rows.reshape(height, breadth, channels)
    padded = jnp.pad(picture, ((1, 1), (1, 1), (0, 0)))
    windows = [
        padded[step_down : step_down + height, step_across : step_across + breadth]
        for step_down in range(3)
        for step_across in range(3)
    ]
    return jnp.concatenate(windows, axis=-1).reshape(height * breadth, 9 * channels)


def unpatch(column_grads, height, breadth):
    channels = column_grads.shape[-1] // 9
    pieces = column_grads.reshape(height, breadth, 9, channels)
    summed = jnp.zeros((height + 2, breadth + 2, channels), jnp.float32)
    for step_down in range(3):
        for step_across in range(3):
            placed = jnp.pad(
                pieces[:, :, 3 * step_down + step_across],
                ((step_down, 2 - step_down), (step_across, 2 - step_across), (0, 0)),
            )
            summed = summed + placed
    return summed[1:-1, 1:-1].reshape(height * breadth, channels)


def attend_scores(queries, key_rows, key_keep, score_scale):
    raw_scores = (
        jnp.einsum("qhd,khd->hqk", queries, key_rows, preferred_element_type=jnp.float32)
        * score_scale
    )
    return jnp.where(key_keep[None, None, :], raw_scores, -1000000000.0)


def split_heads(triple, text_pair, pixel_count, inner_width):
    queries = triple[:, :inner_width].reshape(pixel_count, HEADS, HEAD)
    key_rows = jnp.concatenate(
        [triple[:, inner_width : 2 * inner_width], text_pair[:, :inner_width]], 0
    )
    value_rows = jnp.concatenate([triple[:, 2 * inner_width :], text_pair[:, inner_width:]], 0)
    return (queries, key_rows.reshape(-1, HEADS, HEAD), value_rows.reshape(-1, HEADS, HEAD))


def picture_forward(
    weight_set, pixel_rows, emb_row, text_rows, text_keep, present, height, breadth, score_scale
):
    (
        in_gain,
        in_shift,
        conv_first,
        first_bias,
        emb_weight,
        emb_bias,
        mid_gain,
        mid_shift,
        conv_second,
        second_bias,
        skip_weight,
        skip_bias,
        attn_gain,
        attn_shift,
        attend_weight,
        text_weight,
        out_weight,
        out_bias,
    ) = weight_set
    channels = conv_first.shape[1]
    inner_width = out_weight.shape[0]
    pixel_count = height * breadth
    pixel_float = pixel_rows.astype(jnp.float32)
    first_act = first_activation(
        pixel_float, in_gain.astype(jnp.float32), in_shift.astype(jnp.float32)
    ).astype(jnp.bfloat16)
    first_conv = product(patches(first_act, height, breadth), conv_first) + first_bias.astype(
        jnp.float32
    )
    emb_act = jax.nn.silu(emb_row.astype(jnp.float32)).astype(jnp.bfloat16)[None, :]
    modulation = product(emb_act, emb_weight)[0] + emb_bias.astype(jnp.float32)
    scale_part = modulation[:channels]
    shift_part = modulation[channels:]
    second_act = middle_activation(
        first_conv,
        scale_part,
        shift_part,
        mid_gain.astype(jnp.float32),
        mid_shift.astype(jnp.float32),
    ).astype(jnp.bfloat16)
    residual = (
        product(pixel_rows, skip_weight)
        + skip_bias.astype(jnp.float32)
        + (
            product(patches(second_act, height, breadth), conv_second)
            + second_bias.astype(jnp.float32)
        )
    )
    normed = group_norm(
        residual, attn_gain.astype(jnp.float32), attn_shift.astype(jnp.float32)
    ).astype(jnp.bfloat16)
    triple = product(normed, attend_weight).astype(jnp.bfloat16)
    text_pair = product(text_rows, text_weight).astype(jnp.bfloat16)
    queries, key_rows, value_rows = split_heads(triple, text_pair, pixel_count, inner_width)
    key_keep = jnp.concatenate([jnp.ones((pixel_count,), jnp.bool_), text_keep > 0])
    scores = attend_scores(queries, key_rows, key_keep, score_scale)
    peak_score = jnp.max(scores, axis=-1, keepdims=True)
    exponents = jnp.exp(scores - peak_score)
    denominators = jnp.sum(exponents, axis=-1, keepdims=True)
    attn_probs = (exponents / denominators).astype(jnp.bfloat16)
    log_total = peak_score + jnp.log(denominators)
    attended = jnp.einsum(
        "hqk,khd->qhd", attn_probs, value_rows, preferred_element_type=jnp.float32
    )
    attended = attended.reshape(pixel_count, inner_width).astype(jnp.bfloat16)
    output_rows = present * (
        residual + (product(attended, out_weight) + out_bias.astype(jnp.float32))
    )
    stored = (
        pixel_float,
        first_act,
        first_conv,
        emb_act,
        scale_part,
        shift_part,
        second_act,
        residual,
        normed,
        triple,
        text_pair,
        key_keep,
        log_total,
        attended,
    )
    return (output_rows, stored)


def attention_backward(
    weight_set, stored, grad_out, grad_sums, text_rows, height, breadth, score_scale
):
    attn_gain = weight_set[12]
    attn_shift = weight_set[13]
    attend_weight = weight_set[14]
    out_weight = weight_set[16]
    (
        pixel_float,
        first_act,
        first_conv,
        emb_act,
        scale_part,
        shift_part,
        second_act,
        residual,
        normed,
        triple,
        text_pair,
        key_keep,
        log_total,
        attended,
    ) = stored
    inner_width = out_weight.shape[0]
    pixel_count = height * breadth
    updated = list(grad_sums)
    grad_low = grad_out.astype(jnp.bfloat16)
    updated[17] = updated[17] + jnp.sum(grad_out, axis=0)
    updated[16] = updated[16] + product_left(attended, grad_low)
    grad_attended = product_right(grad_low, out_weight).astype(jnp.bfloat16)
    queries, key_rows, value_rows = split_heads(triple, text_pair, pixel_count, inner_width)
    scores = attend_scores(queries, key_rows, key_keep, score_scale)
    probs_float = jnp.exp(scores - log_total)
    attn_probs = probs_float.astype(jnp.bfloat16)
    grad_heads = grad_attended.reshape(pixel_count, HEADS, HEAD)
    grad_values = jnp.einsum(
        "hqk,qhd->khd", attn_probs, grad_heads, preferred_element_type=jnp.float32
    )
    grad_probs = jnp.einsum(
        "qhd,khd->hqk", grad_heads, value_rows, preferred_element_type=jnp.float32
    )
    grad_scores = probs_float * (
        grad_probs - jnp.sum(grad_probs * probs_float, axis=-1, keepdims=True)
    )
    grad_scores = (grad_scores * score_scale).astype(jnp.bfloat16)
    grad_queries = jnp.einsum(
        "hqk,khd->qhd", grad_scores, key_rows, preferred_element_type=jnp.float32
    )
    grad_keys = jnp.einsum("hqk,qhd->khd", grad_scores, queries, preferred_element_type=jnp.float32)
    grad_keys = grad_keys.reshape(-1, inner_width)
    grad_values = grad_values.reshape(-1, inner_width)
    grad_triple = jnp.concatenate(
        [
            grad_queries.reshape(pixel_count, inner_width),
            grad_keys[:pixel_count],
            grad_values[:pixel_count],
        ],
        1,
    ).astype(jnp.bfloat16)
    grad_text = jnp.concatenate([grad_keys[pixel_count:], grad_values[pixel_count:]], 1).astype(
        jnp.bfloat16
    )
    updated[14] = updated[14] + product_left(normed, grad_triple)
    updated[15] = updated[15] + product_left(text_rows, grad_text)
    grad_normed = product_right(grad_triple, attend_weight)
    _, norm_pull = jax.vjp(
        group_norm, residual, attn_gain.astype(jnp.float32), attn_shift.astype(jnp.float32)
    )
    grad_residual, grad_attn_gain, grad_attn_shift = norm_pull(grad_normed)
    grad_residual = grad_residual + grad_out
    updated[12] = updated[12] + grad_attn_gain
    updated[13] = updated[13] + grad_attn_shift
    return (tuple(updated), grad_residual)


def conv_backward(weight_set, stored, grad_residual, grad_sums, pixel_rows, height, breadth):
    (
        in_gain,
        in_shift,
        conv_first,
        first_bias,
        emb_weight,
        emb_bias,
        mid_gain,
        mid_shift,
        conv_second,
        second_bias,
        skip_weight,
        skip_bias,
    ) = weight_set[:12]
    (
        pixel_float,
        first_act,
        first_conv,
        emb_act,
        scale_part,
        shift_part,
        second_act,
        residual,
        normed,
        triple,
        text_pair,
        key_keep,
        log_total,
        attended,
    ) = stored
    updated = list(grad_sums)
    residual_total = jnp.sum(grad_residual, axis=0)
    updated[9] = updated[9] + residual_total
    updated[11] = updated[11] + residual_total
    residual_low = grad_residual.astype(jnp.bfloat16)
    updated[10] = updated[10] + product_left(pixel_rows, residual_low)
    grad_skip = product_right(residual_low, skip_weight)
    updated[8] = updated[8] + product_left(patches(second_act, height, breadth), residual_low)
    grad_second_act = unpatch(product_right(residual_low, conv_second), height, breadth)
    _, middle_pull = jax.vjp(
        middle_activation,
        first_conv,
        scale_part,
        shift_part,
        mid_gain.astype(jnp.float32),
        mid_shift.astype(jnp.float32),
    )
    grad_first_conv, grad_scale, grad_shift, grad_mid_gain, grad_mid_shift = middle_pull(
        grad_second_act
    )
    updated[6] = updated[6] + grad_mid_gain
    updated[7] = updated[7] + grad_mid_shift
    grad_modulation = jnp.concatenate([grad_scale, grad_shift], 0)
    updated[5] = updated[5] + grad_modulation
    updated[4] = updated[4] + product_left(emb_act, grad_modulation.astype(jnp.bfloat16)[None, :])
    updated[3] = updated[3] + jnp.sum(grad_first_conv, axis=0)
    first_low = grad_first_conv.astype(jnp.bfloat16)
    updated[2] = updated[2] + product_left(patches(first_act, height, breadth), first_low)
    grad_first_act = unpatch(product_right(first_low, conv_first), height, breadth)
    _, first_pull = jax.vjp(
        first_activation, pixel_float, in_gain.astype(jnp.float32), in_shift.astype(jnp.float32)
    )
    grad_pixel_norm, grad_in_gain, grad_in_shift = first_pull(grad_first_act)
    updated[0] = updated[0] + grad_in_gain
    updated[1] = updated[1] + grad_in_shift
    return (tuple(updated), grad_pixel_norm + grad_skip)


def body(
    pixels,
    embedding,
    text_states,
    text_mask,
    occupancy,
    cotangent,
    in_gain,
    in_shift,
    conv_first,
    first_bias,
    emb_weight,
    emb_bias,
    mid_gain,
    mid_shift,
    conv_second,
    second_bias,
    skip_weight,
    skip_bias,
    attn_gain,
    attn_shift,
    attend_weight,
    text_weight,
    out_weight,
    out_bias,
):
    shards = (
        in_gain,
        in_shift,
        conv_first,
        first_bias,
        emb_weight,
        emb_bias,
        mid_gain,
        mid_shift,
        conv_second,
        second_bias,
        skip_weight,
        skip_bias,
        attn_gain,
        attn_shift,
        attend_weight,
        text_weight,
        out_weight,
        out_bias,
    )
    gathered = (
        lax.all_gather(shards[0], "fsdp", axis=0, tiled=True),
        lax.all_gather(shards[1], "fsdp", axis=0, tiled=True),
        lax.all_gather(shards[2], "fsdp", axis=0, tiled=True),
        lax.all_gather(shards[3], "fsdp", axis=0, tiled=True),
        lax.all_gather(shards[4], "fsdp", axis=0, tiled=True),
        lax.all_gather(shards[5], "fsdp", axis=0, tiled=True),
        lax.all_gather(shards[6], "fsdp", axis=0, tiled=True),
        lax.all_gather(shards[7], "fsdp", axis=0, tiled=True),
        lax.all_gather(shards[8], "fsdp", axis=0, tiled=True),
        lax.all_gather(shards[9], "fsdp", axis=0, tiled=True),
        lax.all_gather(shards[10], "fsdp", axis=0, tiled=True),
        lax.all_gather(shards[11], "fsdp", axis=0, tiled=True),
        lax.all_gather(shards[12], "fsdp", axis=0, tiled=True),
        lax.all_gather(shards[13], "fsdp", axis=0, tiled=True),
        lax.all_gather(shards[14], "fsdp", axis=0, tiled=True),
        lax.all_gather(shards[15], "fsdp", axis=0, tiled=True),
        lax.all_gather(shards[16], "fsdp", axis=0, tiled=True),
        lax.all_gather(shards[17], "fsdp", axis=0, tiled=True),
    )
    shapes = ((4 * UNIT, 4 * UNIT), (3 * UNIT, 5 * UNIT), (5 * UNIT, 3 * UNIT))
    score_scale = HEAD ** (-0.5)
    outputs = []
    saved = []
    offset = 0
    for bucket in range(3):
        height, breadth = shapes[bucket]
        present = occupancy[0, bucket].astype(jnp.float32)
        output_rows, stored = picture_forward(
            gathered,
            pixels[offset : offset + height * breadth],
            embedding[bucket],
            text_states[bucket],
            text_mask[bucket],
            present,
            height,
            breadth,
            score_scale,
        )
        outputs.append(output_rows)
        saved.append(stored)
        offset += height * breadth
    block_output = jnp.concatenate(outputs, 0).astype(jnp.bfloat16)
    back_set = (
        lax.all_gather(shards[0], "fsdp", axis=0, tiled=True),
        lax.all_gather(shards[1], "fsdp", axis=0, tiled=True),
        lax.all_gather(shards[2], "fsdp", axis=0, tiled=True),
        lax.all_gather(shards[3], "fsdp", axis=0, tiled=True),
        lax.all_gather(shards[4], "fsdp", axis=0, tiled=True),
        lax.all_gather(shards[5], "fsdp", axis=0, tiled=True),
        lax.all_gather(shards[6], "fsdp", axis=0, tiled=True),
        lax.all_gather(shards[7], "fsdp", axis=0, tiled=True),
        lax.all_gather(shards[8], "fsdp", axis=0, tiled=True),
        lax.all_gather(shards[9], "fsdp", axis=0, tiled=True),
        lax.all_gather(shards[10], "fsdp", axis=0, tiled=True),
        lax.all_gather(shards[11], "fsdp", axis=0, tiled=True),
        lax.all_gather(shards[12], "fsdp", axis=0, tiled=True),
        lax.all_gather(shards[13], "fsdp", axis=0, tiled=True),
        lax.all_gather(shards[14], "fsdp", axis=0, tiled=True),
        lax.all_gather(shards[15], "fsdp", axis=0, tiled=True),
        lax.all_gather(shards[16], "fsdp", axis=0, tiled=True),
        lax.all_gather(shards[17], "fsdp", axis=0, tiled=True),
    )
    grad_sums = tuple((jnp.zeros(member.shape, jnp.float32) for member in back_set))
    starts = (0, 16 * UNIT * UNIT, 31 * UNIT * UNIT)
    pixel_grads = []
    for bucket in range(3):
        height, breadth = shapes[bucket]
        begin = starts[bucket]
        present = occupancy[0, bucket].astype(jnp.float32)
        grad_out = cotangent[begin : begin + height * breadth].astype(jnp.float32) * present
        grad_sums, grad_residual = attention_backward(
            back_set,
            saved[bucket],
            grad_out,
            grad_sums,
            text_states[bucket],
            height,
            breadth,
            score_scale,
        )
        grad_sums, grad_rows = conv_backward(
            back_set,
            saved[bucket],
            grad_residual,
            grad_sums,
            pixels[begin : begin + height * breadth],
            height,
            breadth,
        )
        pixel_grads.append(grad_rows)
    owned = jax.tree.map(
        lambda part: part.astype(jnp.float32),
        lax.psum_scatter(for_sending(grad_sums), "fsdp", scatter_dimension=0, tiled=True),
    )
    replicated = tuple(
        jax.tree.map(lambda part: part.astype(jnp.float32), lax.psum(for_sending(owned), "dp"))
    )
    return (block_output, jnp.concatenate(pixel_grads, 0)) + tuple(replicated)


def solution(mesh):
    return jax.shard_map(
        body,
        mesh=mesh,
        in_specs=(
            P(("dp", "fsdp"), None),
            P(("dp", "fsdp"), None),
            P(("dp", "fsdp"), None, None),
            P(("dp", "fsdp"), None),
            P(("dp", "fsdp"), None),
            P(("dp", "fsdp"), None),
            P("fsdp"),
            P("fsdp"),
            P("fsdp", None),
            P("fsdp"),
            P("fsdp", None),
            P("fsdp"),
            P("fsdp"),
            P("fsdp"),
            P("fsdp", None),
            P("fsdp"),
            P("fsdp", None),
            P("fsdp"),
            P("fsdp"),
            P("fsdp"),
            P("fsdp", None),
            P("fsdp", None),
            P("fsdp", None),
            P("fsdp"),
        ),
        out_specs=(
            P(("dp", "fsdp"), None),
            P(("dp", "fsdp"), None),
            P("fsdp"),
            P("fsdp"),
            P("fsdp", None),
            P("fsdp"),
            P("fsdp", None),
            P("fsdp"),
            P("fsdp"),
            P("fsdp"),
            P("fsdp", None),
            P("fsdp"),
            P("fsdp", None),
            P("fsdp"),
            P("fsdp"),
            P("fsdp"),
            P("fsdp", None),
            P("fsdp", None),
            P("fsdp", None),
            P("fsdp"),
        ),
        check_vma=False,
    )
```

profile of v0, /device:TPU:0, one launch (start us, length us, event | category | flops | bytes accessed | tf_op | source)
XLA Modules:
  0.0 1537.9 jit_solution(1004383911731375751)
XLA Ops:
  20.6 63.2 %all-reduce.84 = (bf16[512]{0:T(512)(128)(2,1)S(1)}, bf16[512]{0:T(512)(128)(2,1)S(1)}, bf16[1024]{0:T(1024)(128)(2,1)S(1)}, bf16[1024]{0:T(1024)(128)(2,1)S(1)}...) all-reduce(bf16[512]{0:T(512)(128)(2,1)S(1)} %dynamic-update-slice., ...), channel_id=1, replica_groups=mesh['dp'=2,'fsdp'=16] {'fsdp'}, use_global_device_ids=true, to_apply=%add.65 | all-reduce | flops 8192 | bytes 32768
  87.9 17.2 %all-gather = bf16[16,1,128]{2,1,0:T(2,128)(2,1)S(1)} all-gather(bf16[1,1,128]{2,1,0:T(2,128)(2,1)S(1)} %bitcast.526), channel_id=1, replica_groups=mesh['dp'=2,'fsdp'=16] {'fsdp'}, dimensions={0}, use_global_device_ids=true | all-gather | bytes 4352 | tf_op jit(solution)/shard_map/all_gather | solution.py:385
  166.3 4.7 fusion.258
  174.5 67.0 %all-gather.19.cloned.1.call-done = bf16[4096,1024]{1,0:T(8,128)(2,1)} async-done(((bf16[256,1024]{1,0:T(8,128)(2,1)}), bf16[4096,1024]{1,0:T(8,128)(2,1)}) %all-gather.19.cloned.1.call-update) | async-done | bytes 8388624 | tf_op jit(solution)/shard_map/all_gather | solution.py:395
  241.5 5.1 convolution_convert_fusion.6
  252.2 71.2 %all-gather.11.cloned.1.call-done = bf16[4608,1024]{1,0:T(8,128)(2,1)} async-done(((bf16[288,1024]{1,0:T(8,128)(2,1)}), bf16[4608,1024]{1,0:T(8,128)(2,1)}) %all-gather.11.cloned.1.call-update) | async-done | bytes 9437200 | tf_op jit(solution)/shard_map/all_gather | solution.py:382
  323.4 6.8 fusion.336
  331.5 6.8 fusion.337
  344.2 6.6 fusion.342
  415.4 6.6 all-gather.15.cloned.1.call-done
  422.0 10.3 convolution_add_fusion.8
  434.0 35.4 %all-gather.17.cloned.1.call-done = bf16[1024,1536]{1,0:T(8,128)(2,1)} async-done(((bf16[64,1536]{1,0:T(8,128)(2,1)}), bf16[1024,1536]{1,0:T(8,128)(2,1)}) %all-gather.17.cloned.1.call-update) | async-done | bytes 3145744 | tf_op jit(solution)/shard_map/all_gather | solution.py:394
  484.5 6.1 fusion.113
  490.6 6.1 fusion.101
  499.7 10.3 convolution_add_fusion.7
  523.0 6.2 fusion.110
  529.2 6.3 fusion.104
  537.8 10.9 fusion.343
  562.1 6.2 fusion.116
  568.3 6.2 fusion.98
  613.9 11.2 fusion.349
  625.1 11.6 reshape.909
  636.7 28.1 %fusion.324 = (f32[12,20,1,1024]{3,2,1,0:T(1,128)}, f32[12,20,1,1024]{3,2,1,0:T(1,128)}, f32[12,20,1,1024]{3,2,1,0:T(1,128)}, f32[12,20,1,1024]{3,2,1,0:T(1,128)...) fusion(f32[12,20,9,1024]{3,2,1,0:T(8,128)} %reshape.909), kind=kLoop, calls=%fused_computation.655 | loop fusion | bytes 17694720 | tf_op jit(solution)/shard_map/slice | solution.py:74
  674.9 11.1 fusion.351
  685.9 11.5 reshape.914
  697.4 29.3 %fusion.325 = (f32[20,12,1,1024]{3,2,1,0:T(1,128)}, f32[20,12,1,1024]{3,2,1,0:T(1,128)}, f32[20,12,1,1024]{3,2,1,0:T(1,128)}, f32[20,12,1,1024]{3,2,1,0:T(1,128)...) fusion(f32[20,12,9,1024]{3,2,1,0:T(8,128)} %reshape.914), kind=kLoop, calls=%fused_computation.656 | loop fusion | bytes 17694720 | tf_op jit(solution)/shard_map/slice | solution.py:74
  744.7 5.1 multiply_reduce_fusion.16
  759.5 11.3 fusion.346
  771.0 12.6 reshape.904
  789.8 28.3 %fusion.323 = (f32[16,16,1,1024]{3,2,1,0:T(1,128)S(1)}, f32[16,16,1,1024]{3,2,1,0:T(1,128)S(1)}, f32[16,16,1,1024]{3,2,1,0:T(1,128)S(1)}, f32[16,16,1,1024]{3,2,...) fusion(f32[16,16,9,1024]{3,2,1,0:T(8,128)} %reshape.904), kind=kLoop, calls=%fused_computation.654 | loop fusion | bytes 18874368 | tf_op jit(solution)/shard_map/slice | solution.py:74
  829.1 5.5 add_convert_fusion.3
  840.4 8.3 fusion.149
  848.7 8.0 fusion.146
  856.7 15.6 %fusion.3 = bf16[4096,1024]{0,1:T(8,128)(2,1)} fusion(f32[1024,4096]{1,0:T(8,128)} %fusion.149, f32[1024,4096]{1,0:T(8,128)} %fusion.146, bf16[3,77,4096]{2,1,0:T(8,128)(2,1)S(1)} %copy-done.24, bf16[77,512]{0,1:T(8,128)(2,1)S(1)} %bitcast.513, bf16[77,512]{0,1:T(8,128)(2,1)S(1)} %bitcast.514), kind=kOutput, calls=%fused_computation.7 | convolution fusion | flops 658821120 | bytes 42860544 | tf_op jit(solution)/shard_map/dot_general | solution.py:25
  872.4 9.7 fusion.353
  882.1 9.7 fusion.352
  891.8 21.4 %add_convert_fusion.1 = bf16[4608,1024]{1,0:T(8,128)(2,1)} fusion(f32[4608,1024]{1,0:T(8,128)} %fusion.352, f32[4608,1024]{1,0:T(8,128)} %fusion.353, bf16[240,4608]{1,0:T(8,128)(2,1)} %constant_dynamic-update-slice_fusion.36, bf16[240,1024]{1,0:T(8,128)(2,1)S(1)} %copy-done.41), kind=kOutput, calls=%fused_computation.4 | convolution fusion | flops 2279079936 | bytes 49889280 | tf_op jit(solution)/shard_map/dot_general | solution.py:25
  914.2 17.2 %fusion.355 = f32[9216,1024]{1,0:T(8,128)} fusion(bf16[240,9216]{1,0:T(8,128)(2,1)} %constant_dynamic-update-slice_fusion.45, bf16[240,1024]{1,0:T(8,128)(2,1)S(1)} %copy-done.31), kind=kOutput, calls=%fused_computation.686 | convolution fusion | flops 4529848320 | bytes 42663936 | tf_op jit(solution)/shard_map/dot_general | solution.py:25
  931.4 17.4 %fusion.354 = f32[9216,1024]{1,0:T(8,128)} fusion(bf16[240,9216]{1,0:T(8,128)(2,1)} %constant_dynamic-update-slice_fusion.27, bf16[240,1024]{1,0:T(8,128)(2,1)S(1)} %copy-done.27), kind=kOutput, calls=%fused_computation.685 | convolution fusion | flops 4529848320 | bytes 42663936 | tf_op jit(solution)/shard_map/dot_general | solution.py:25
  948.8 34.2 %add_convert_fusion = bf16[9216,1024]{1,0:T(8,128)(2,1)} fusion(f32[9216,1024]{1,0:T(8,128)} %fusion.355, f32[9216,1024]{1,0:T(8,128)} %fusion.354, bf16[256,9216]{1,0:T(8,128)(2,1)} %constant_dynamic-update-slice_fusion.9, bf16[256,1024]{1,0:T(8,128)(2,1)S(1)} %get-tuple-element.442), kind=kOutput, calls=%fused_computation.3 | convolution fusion | flops 4860149760 | bytes 99614720 | tf_op jit(solution)/shard_map/dot_general | solution.py:25
  986.4 6.0 fusion.164
  995.0 5.7 fusion.166
  1007.3 6.2 fusion.347
  1024.0 76.9 %reduce-scatter.18.cloned.1.call-done = bf16[256,1024]{0,1:T(8,128)(2,1)} async-done(((bf16[4096,1024]{0,1:T(8,128)(2,1)}), bf16[256,1024]{0,1:T(8,128)(2,1)}) %reduce-scatter.18.cloned.1.call-update) | async-done | bytes 524304 | tf_op jit(solution)/shard_map/reduce_scatter | solution.py:472
  1101.0 115.2 %reduce-scatter.10.cloned.1.call-done = bf16[288,1024]{1,0:T(8,128)(2,1)} async-done(((bf16[4608,1024]{1,0:T(8,128)(2,1)}), bf16[288,1024]{1,0:T(8,128)(2,1)}) %reduce-scatter.10.cloned.1.call-update) | async-done | bytes 589840 | tf_op jit(solution)/shard_map/reduce_scatter | solution.py:472
  1216.2 199.3 %reduce-scatter.14.cloned.1.call-done = bf16[576,1024]{1,0:T(8,128)(2,1)} async-done(((bf16[9216,1024]{1,0:T(8,128)(2,1)}), bf16[576,1024]{1,0:T(8,128)(2,1)}) %reduce-scatter.14.cloned.1.call-update) | async-done | bytes 1179664 | tf_op jit(solution)/shard_map/reduce_scatter | solution.py:472
  1420.3 59.9 %all-reduce.83 = (bf16[1024]{0:T(1024)(128)(2,1)S(1)}, bf16[512]{0:T(512)(128)(2,1)}, bf16[512]{0:T(512)(128)(2,1)S(1)}, bf16[1024]{0:T(1024)(128)(2,1)S(1)}, bf...) all-reduce(bf16[1024]{0:T(1024)(128)(2,1)} %copy-done.247, ...), channel_id=1, replica_groups=mesh['dp'=2,'fsdp'=16] {'fsdp'}, use_global_device_ids=true, to_apply=%add.72 | all-reduce | flops 11264 | bytes 45056
  1488.2 5.8 all-reduce.85
  (1161 shorter events, 373.6 us)
Async XLA Ops:
  7.3 12.8 copy-start.283
  7.3 13.0 copy-start.284
  7.3 80.6 %copy-start.257 = (bf16[128]{0:T(256)(128)(2,1)S(1)}, bf16[128]{0:T(256)(128)(2,1)}, u32[]{:S(2)}) copy-start(bf16[128]{0:T(256)(128)(2,1)} %param.35) | copy-start | bytes 772
  7.3 98.4 %copy-start.127 = (bf16[3,2048]{1,0:T(4,128)(2,1)S(1)}, bf16[3,2048]{1,0:T(4,128)(2,1)}, u32[]{:S(2)}) copy-start(bf16[3,2048]{1,0:T(4,128)(2,1)} %param.25) | copy-start | bytes 36868
  7.4 146.9 %all-gather.21.cloned.1.call-start = ((), (), s32[]{:S(2)}) async-start(), calls=%async_computation.13 | async-start | bytes 1114112 | tf_op jit(solution)/shard_map/all_gather | solution.py:396
  8.1 152.4 %all-gather.9.cloned.1.call-start = ((), (), s32[]{:S(2)}) async-start(), calls=%async_computation.7 | async-start | bytes 1114112 | tf_op jit(solution)/shard_map/all_gather | solution.py:390
  8.8 157.5 %all-gather.13.cloned.1.call-start = ((), (), s32[]{:S(2)}) async-start(), calls=%async_computation.9 | async-start | bytes 8912896 | tf_op jit(solution)/shard_map/all_gather | solution.py:384
  9.6 231.9 %all-gather.19.cloned.1.call-start = ((), (), s32[]{:S(2)}) async-start(), calls=%async_computation.12 | async-start | bytes 8912896 | tf_op jit(solution)/shard_map/all_gather | solution.py:395
  10.1 313.2 %all-gather.11.cloned.1.call-start = ((), (), s32[]{:S(2)}) async-start(), calls=%async_computation.8 | async-start | bytes 10027008 | tf_op jit(solution)/shard_map/all_gather | solution.py:382
  10.7 411.2 %all-gather.15.cloned.1.call-start = ((), (), s32[]{:S(2)}) async-start(), calls=%async_computation.10 | async-start | bytes 20054016 | tf_op jit(solution)/shard_map/all_gather | solution.py:388
  11.3 458.1 %all-gather.17.cloned.1.call-start = ((), (), s32[]{:S(2)}) async-start(), calls=%async_computation.11 | async-start | bytes 3342336 | tf_op jit(solution)/shard_map/all_gather | solution.py:394
  12.1 1010.3 %reduce-scatter.22.cloned.1.call-start = ((), (), s32[]{:S(2)}) async-start(), calls=%async_computation.20 | async-start | bytes 1114112
  83.8 28.4 %copy-start.168 = (f32[512]{0:T(512)}, f32[512]{0:T(512)S(1)}, u32[]{:S(2)}) copy-start(f32[512]{0:T(512)S(1)} %convert_element_type.567) | copy-start | bytes 6148
  83.8 28.4 %copy-start.150 = (f32[512]{0:T(512)}, f32[512]{0:T(512)S(1)}, u32[]{:S(2)}) copy-start(f32[512]{0:T(512)S(1)} %convert_element_type.566) | copy-start | bytes 6148
  173.3 68.2 %copy-start.23 = (bf16[3,77,4096]{2,1,0:T(8,128)(2,1)S(1)}, bf16[3,77,4096]{2,1,0:T(8,128)(2,1)}, u32[]{:S(2)}) copy-start(bf16[3,77,4096]{2,1,0:T(8,128)(2,1)} %param.26) | copy-start | bytes 5677060
  174.5 236.1 %copy-start.159 = (f32[1024]{0:T(1024)}, f32[1024]{0:T(1024)S(1)}, u32[]{:S(2)}) copy-start(f32[1024]{0:T(1024)S(1)} %get-tuple-element.514) | copy-start | bytes 12292
  174.5 236.1 %copy-start.174 = (f32[1024]{0:T(1024)}, f32[1024]{0:T(1024)S(1)}, u32[]{:S(2)}) copy-start(f32[1024]{0:T(1024)S(1)} %get-tuple-element.513) | copy-start | bytes 12292
  249.8 73.5 %copy-start.253 = (f32[1024]{0:T(1024)S(1)}, f32[1024]{0:T(1024)}, u32[]{:S(2)}) copy-start(f32[1024]{0:T(1024)} %convert_element_type.569) | copy-start | bytes 12292
  252.1 87.5 %copy-start.181 = (f32[1024]{0:T(1024)}, f32[1024]{0:T(1024)S(1)}, u32[]{:S(2)}) copy-start(f32[1024]{0:T(1024)S(1)} %get-tuple-element.555) | copy-start | bytes 12292
  252.1 87.5 %copy-start.184 = (f32[1024]{0:T(1024)}, f32[1024]{0:T(1024)S(1)}, u32[]{:S(2)}) copy-start(f32[1024]{0:T(1024)S(1)} %get-tuple-element.522) | copy-start | bytes 12292
  252.1 87.5 %copy-start.196 = (f32[1024]{0:T(1024)}, f32[1024]{0:T(1024)S(1)}, u32[]{:S(2)}) copy-start(f32[1024]{0:T(1024)S(1)} %get-tuple-element.523) | copy-start | bytes 12292
  252.1 87.5 %copy-start.206 = (f32[1024]{0:T(1024)}, f32[1024]{0:T(1024)S(1)}, u32[]{:S(2)}) copy-start(f32[1024]{0:T(1024)S(1)} %get-tuple-element.554) | copy-start | bytes 12292
  350.8 59.8 %copy-start.8 = (f32[256,1024]{1,0:T(8,128)}, f32[256,1024]{1,0:T(8,128)S(1)}, u32[]{:S(2)}) copy-start(f32[256,1024]{1,0:T(8,128)S(1)} %get-tuple-element.546) | copy-start | bytes 3145732
  351.2 59.5 %copy-start.148 = (f32[1024]{0:T(1024)}, f32[1024]{0:T(1024)S(1)}, u32[]{:S(2)}) copy-start(f32[1024]{0:T(1024)S(1)} %sub.180) | copy-start | bytes 12292
  370.1 40.5 %copy-start.157 = (f32[1024]{0:T(1024)}, f32[1024]{0:T(1024)S(1)}, u32[]{:S(2)}) copy-start(f32[1024]{0:T(1024)S(1)} %mul.935) | copy-start | bytes 12292
  415.4 16.9 %copy-start.6 = (bf16[512,1024]{1,0:T(8,128)(2,1)S(1)}, bf16[512,1024]{1,0:T(8,128)(2,1)}, u32[]{:S(2)}) copy-start(bf16[512,1024]{1,0:T(8,128)(2,1)} %all-gather.9.cloned.1.call-done) | copy-start | bytes 3145732
  432.2 37.2 %copy-start.129 = (f32[1024]{0:T(1024)S(1)}, f32[1024]{0:T(1024)}, u32[]{:S(2)}) copy-start(f32[1024]{0:T(1024)} %convert_element_type.577) | copy-start | bytes 12292
  432.2 37.2 %copy-start.132 = (f32[1024]{0:T(1024)S(1)}, f32[1024]{0:T(1024)}, u32[]{:S(2)}) copy-start(f32[1024]{0:T(1024)} %convert_element_type.578) | copy-start | bytes 12292
  432.7 350.9 %copy-start.4 = (f32[240,1024]{1,0:T(8,128)}, f32[240,1024]{1,0:T(8,128)S(1)}, u32[]{:S(2)}) copy-start(f32[240,1024]{1,0:T(8,128)S(1)} %get-tuple-element.541) | copy-start | bytes 2949124
  513.5 94.6 %copy-start.189 = (f32[1024]{0:T(1024)}, f32[1024]{0:T(1024)S(1)}, u32[]{:S(2)}) copy-start(f32[1024]{0:T(1024)S(1)} %mul.995) | copy-start | bytes 12292
  537.8 43.0 %copy-start.83 = (bf16[317,8,64]{0,2,1:T(8,128)(2,1)}, bf16[317,8,64]{0,2,1:T(8,128)(2,1)S(1)}, u32[]{:S(2)}) copy-start(bf16[317,8,64]{0,2,1:T(8,128)(2,1)S(1)} %fusion.122) | copy-start | bytes 973828
  613.9 410.2 %reduce-scatter.20.cloned.1.call-start = ((), (), s32[]{:S(2)}) async-start(), calls=%async_computation.19 | async-start | bytes 1114112 | tf_op jit(solution)/shard_map/reduce_scatter | solution.py:472
  759.4 264.6 %reduce-scatter.16.cloned.1.call-start = ((), (), s32[]{:S(2)}) async-start(), calls=%async_computation.17 | async-start | bytes 3342336 | tf_op jit(solution)/shard_map/reduce_scatter | solution.py:472
  789.7 234.3 %reduce-scatter.12.cloned.1.call-start = ((), (), s32[]{:S(2)}) async-start(), calls=%async_computation.15 | async-start | bytes 8912896 | tf_op jit(solution)/shard_map/reduce_scatter | solution.py:472
  834.7 266.3 %reduce-scatter.18.cloned.1.call-start = ((), (), s32[]{:S(2)}) async-start(), calls=%async_computation.18 | async-start | bytes 8912896 | tf_op jit(solution)/shard_map/reduce_scatter | solution.py:472
  872.4 343.8 %reduce-scatter.10.cloned.1.call-start = ((), (), s32[]{:S(2)}) async-start(), calls=%async_computation.14 | async-start | bytes 10027008 | tf_op jit(solution)/shard_map/reduce_scatter | solution.py:472
  913.2 18.2 %copy-start.27 = (bf16[240,1024]{1,0:T(8,128)(2,1)S(1)}, bf16[240,1024]{1,0:T(8,128)(2,1)}, u32[]{:S(2)}) copy-start(bf16[240,1024]{1,0:T(8,128)(2,1)} %copy-done.25) | copy-start | bytes 1474564
  913.2 502.2 %reduce-scatter.14.cloned.1.call-start = ((), (), s32[]{:S(2)}) async-start(), calls=%async_computation.16 | async-start | bytes 20054016 | tf_op jit(solution)/shard_map/reduce_scatter | solution.py:472
  983.0 536.4 %all-reduce.89.cloned.1.call-start = ((), (), s32[]{:S(2)}) async-start(), calls=%async_computation.21 | async-start | bytes 6684672 | tf_op jit(solution)/shard_map/psum | solution.py:475
  1016.3 399.2 %copy-start.199 = (f32[1024]{0:T(1024)S(1)}, f32[1024]{0:T(1024)}, u32[]{:S(2)}) copy-start(f32[1024]{0:T(1024)} %copy-done.198) | copy-start | bytes 12292
  1016.3 399.2 %copy-start.201 = (f32[1024]{0:T(1024)S(1)}, f32[1024]{0:T(1024)}, u32[]{:S(2)}) copy-start(f32[1024]{0:T(1024)} %copy-done.200) | copy-start | bytes 12292
  1016.4 399.2 %copy-start.203 = (f32[1024]{0:T(1024)S(1)}, f32[1024]{0:T(1024)}, u32[]{:S(2)}) copy-start(f32[1024]{0:T(1024)} %copy-done.202) | copy-start | bytes 12292
  1016.4 399.2 %copy-start.205 = (f32[1024]{0:T(1024)S(1)}, f32[1024]{0:T(1024)}, u32[]{:S(2)}) copy-start(f32[1024]{0:T(1024)} %copy-done.204) | copy-start | bytes 12292
  1016.4 399.2 %copy-start.209 = (f32[1024]{0:T(1024)S(1)}, f32[1024]{0:T(1024)}, u32[]{:S(2)}) copy-start(f32[1024]{0:T(1024)} %get-tuple-element.290) | copy-start | bytes 12292
  1016.4 399.2 %copy-start.211 = (f32[1024]{0:T(1024)S(1)}, f32[1024]{0:T(1024)}, u32[]{:S(2)}) copy-start(f32[1024]{0:T(1024)} %get-tuple-element.324) | copy-start | bytes 12292
  1016.4 495.8 %copy-start.11 = (f32[240,1024]{1,0:T(8,128)S(1)}, f32[240,1024]{1,0:T(8,128)}, u32[]{:S(2)}) copy-start(f32[240,1024]{1,0:T(8,128)} %get-tuple-element.537) | copy-start | bytes 2949124
  1415.5 98.7 %copy-start.5 = (f32[240,1024]{1,0:T(8,128)S(1)}, f32[240,1024]{1,0:T(8,128)}, u32[]{:S(2)}) copy-start(f32[240,1024]{1,0:T(8,128)} %copy-done.4) | copy-start | bytes 2949124
  1415.5 98.7 %copy-start.95 = (bf16[8,64,240]{2,1,0:T(8,128)(2,1)S(1)}, bf16[8,64,240]{2,1,0:T(8,128)(2,1)}, u32[]{:S(2)}) copy-start(bf16[8,64,240]{2,1,0:T(8,128)(2,1)} %fusion.108) | copy-start | bytes 737284
  (255 other events, 1124.3 us)
Sparse Core Ops, SparseCore 0:
  10.3 40.8 all-gather.20
  53.4 36.8 all-gather.8
  92.5 73.8 all-gather.12
  168.3 73.1 all-gather.18
  243.6 79.6 all-gather.10
  324.8 97.0 all-gather.14
  424.2 45.1 all-gather.16
  614.0 56.2 reduce-scatter.21
  759.6 56.1 reduce-scatter.19
  819.4 65.2 reduce-scatter.15
  888.8 103.5 reduce-scatter.11
  996.3 104.5 reduce-scatter.17
  1105.1 111.0 reduce-scatter.9
  1220.7 194.7 reduce-scatter.13
  1418.2 90.3 all-reduce.88
where the time goes:
time: 1550 us; the launch traced here: 1540 us
  waiting for transfers between devices  579 us (37%)
  matrix products  362 us (23%)
  local copies, waits for them, and re-layouts  325 us (21%)
  blocking collectives  146 us (9%)
  other arithmetic  101 us (7%)
  between operations  23.1 us (1%)
    reduce_scatter x6, waiting for transfers between devices, body(): lax.psum_scatter(for_sending(grad_sums), 'fsdp', scatter_dimension=0, til...  391 us
    dot_general x18, matrix products, product_left(): lax.dot_general(first_operand, second_operand, (((0,), (0,)), ((), ())),...  156 us
    unnamed x2, blocking collectives  123 us
    slice x12, local copies, waits for them, and re-layouts, unpatch(): pieces[:, :, 3 * step_down + step_across]  92.2 us
    unnamed x673, local copies, waits for them, and re-layouts  84 us
    dot_general x21, matrix products, product(): jnp.dot(first_operand, second_operand, preferred_element_type=jnp.float32)  83.6 us
    all_gather x1, waiting for transfers between devices, body(): lax.all_gather(shards[2], 'fsdp', axis=0, tiled=True)  71.2 us
    all_gather x1, waiting for transfers between devices, body(): lax.all_gather(shards[15], 'fsdp', axis=0, tiled=True)  67 us
  transfers between devices with their start and end apart: 15, of which 8 were waited for; matrix products, arithmetic and copies ran while one was open for 40% of the time, Pallas kernels for 0%

commit v1 on v0

v1 whole, which is shorter than its diff:
```python
import functools

import jax
import jax.numpy as jnp
from jax import lax
from jax.experimental import pallas as pl
from jax.experimental.pallas import tpu as pltpu
from jax.sharding import PartitionSpec as P

MESH = pl.DeviceIdType.MESH
BF16=jnp.bfloat16
DEPTH = 4


class Where:
    def __init__(self, replicas, parts):
        self.replicas, self.parts = replicas, parts
        self.span = parts // (2 * DEPTH)
        self.group = lax.axis_index("dp")
        self.place = lax.axis_index("fsdp")
        self.core = lax.rem(self.place, 2)
        self.y = lax.rem(self.place // 2, self.span)
        self.z = self.place // (2 * self.span)
        self.side = lax.rem(self.group, 2)

    def index(self, z, y, core):
        return (z * self.span + y) * 2 + core

    def device(self, z=None, y=None, core=None, flip=False):
        z = self.z if z is None else z
        y = self.y if y is None else y
        core = self.core if core is None else core
        group = self.group + 1 - 2 * self.side if flip else self.group
        return (group, self.index(z, y, core))

    def barrier(self):
        sem = pltpu.get_barrier_semaphore()
        greet = lambda device: pl.semaphore_signal(sem, inc=1, device_id=device, device_id_type=MESH)
        greet(self.device(flip=True))
        def one(i, carry):
            greet((self.group, lax.rem(self.place + i, self.parts)))
            return carry
        lax.fori_loop(1, self.parts, one, 0)
        pl.semaphore_wait(sem, self.parts)


def gather_kernel(replicas, parts, rows, lead, own, note, emb, full, mod, notes, part, sums, n_send, n_recv, m_send, m_recv, z_send, z_recv, y_send, y_recv, s_send, s_recv, x_send, x_recv, c_send, c_recv, own_sem):
    me = Where(replicas, parts)
    span = me.span
    total, width = own.shape
    chunks = total // rows
    half = width // 2
    side = me.side
    thin = 128
    z_cols = pl.ds(pl.multiple_of(side * thin, thin), width - thin)
    a_cols = pl.ds(pl.multiple_of(side * half, half), half)
    thin_cols = pl.ds(pl.multiple_of((1 - side) * (width - thin), thin), thin)
    thin_out = pl.ds(pl.multiple_of(side * (width - thin), thin), thin)
    b_cols = pl.ds(pl.multiple_of((1 - side) * half, half), half)

    me.barrier()
    local = pltpu.make_async_copy(own, full.at[me.place], own_sem)
    local.start()

    def at(k):
        return pl.ds(pl.multiple_of(k * rows, 16), rows)

    def copy(src, dst, send, recv, device):
        return pltpu.make_async_remote_copy(src_ref=src, dst_ref=dst, send_sem=send, recv_sem=recv, device_id=device, device_id_type=MESH)

    def piece(k, z, y, cols, core=None):
        return full.at[me.index(z, y, me.core if core is None else core), at(k), cols]

    def z_copy(k, z, step, mine):
        src = own.at[at(k), z_cols] if mine else piece(k, z, me.y, z_cols)
        return copy(src, piece(k, z, me.y, z_cols), z_send.at[k, z, (step + 1) // 2], z_recv.at[k, z], me.device(z=me.z + step))

    def y_copy(k, z, turn, mine):
        src = own.at[at(k), a_cols] if mine else piece(k, z, me.y, a_cols)
        return copy(src, piece(k, z, me.y, a_cols), y_send.at[k, z, turn - 1], y_recv.at[k, z, turn - 1], me.device(y=lax.rem(me.y + turn, span)))

    def thin_copy(k, z):
        return copy(piece(k, z, me.y, thin_out), piece(k, z, me.y, thin_out), s_send.at[k, z], s_recv.at[k, z], me.device(flip=True))

    def x_copy(k, z, turn):
        y = lax.rem(me.y + turn, span)
        return copy(piece(k, z, y, a_cols), piece(k, z, y, a_cols), x_send.at[k, z, turn - 1], x_recv.at[k, z, turn - 1], me.device(flip=True))

    def core_copy(k, z, y, cols, mine=False):
        src = own.at[at(k), cols] if mine else piece(k, z, y, cols)
        return copy(src, piece(k, z, y, cols), c_send.at[k], c_recv.at[k], me.device(core=1 - me.core))

    everything = pl.ds(0, width)
    below = lambda s: (me.z - s >= 0, me.z - s)
    above = lambda s: (me.z + s < DEPTH, me.z + s)

    def start_own(k):
        @pl.when(me.z < DEPTH - 1)
        def _():
            z_copy(k, me.z, 1, True).start()
        @pl.when(me.z > 0)
        def _():
            z_copy(k, me.z, -1, True).start()
        for turn in range(1, span):
            y_copy(k, me.z, turn, True).start()
        core_copy(k, me.z, me.y, everything, True).start()

    def along_z(k, s):
        for (ok, z), step in ((below(s), 1), (above(s), -1)):
            @pl.when(ok)
            def _():
                z_copy(k, z, step, False).wait_recv()
                if s < DEPTH - 1:
                    more = me.z < DEPTH - 1 if step > 0 else me.z > 0
                    @pl.when(more)
                    def _():
                        z_copy(k, z, step, False).start()
                for turn in range(1, span):
                    y_copy(k, z, turn, False).start()
                thin_copy(k, z).start()
                core_copy(k, z, me.y, z_cols).start()

    def across(k, s):
        for ok, z in ((below(s), above(s)) if s else (below(0),)):
            @pl.when(ok)
            def _():
                for turn in range(1, span):
                    y_copy(k, z, turn, False).wait_recv()
                    x_copy(k, z, span - turn).start()
                    core_copy(k, z, lax.rem(me.y + span - turn, span), a_cols).start()

    def beside(k, s):
        for ok, z in ((below(s), above(s)) if s else (below(0),)):
            @pl.when(ok)
            def _():
                for turn in range(1, span):
                    x_copy(k, z, turn).wait_recv()
                    core_copy(k, z, lax.rem(me.y + turn, span), b_cols).start()

    def beside_thin(k, s):
        for ok, z in (below(s), above(s)):
            @pl.when(ok)
            def _():
                thin_copy(k, z).wait_recv()
                core_copy(k, z, me.y, thin_cols).start()

    for k in range(min(lead, chunks)):
        start_own(k)

    last = 2 * (DEPTH - 1) + 3

    def slot(t, carry):
        def stage(delay, work):
            k = t - delay
            @pl.when(jnp.logical_and(k >= 0, k < chunks))
            def _():
                work(k)
        @pl.when(t + lead < chunks)
        def _():
            start_own(t + lead)
        for s in range(1, DEPTH):
            stage(s - 1, functools.partial(along_z, s=s))
        for s in range(DEPTH):
            stage(s + 0, functools.partial(across, s=s))
        for s in range(1, DEPTH):
            stage(s + 0, functools.partial(beside_thin, s=s))
        for s in range(DEPTH):
            stage(s + 1, functools.partial(beside, s=s))
        return carry

    def to_all(make):
        def one(i, carry):
            make(lax.rem(me.place + i, parts)).start()
            return carry
        lax.fori_loop(1, parts, one, 0)

    def wait_all(ref, send, recv):
        others = ref.at[pl.ds(0, parts - 1)]
        every = copy(others, others, send, recv, me.device(core=1 - me.core))
        every.wait_send()
        every.wait_recv()

    to_all(lambda far: copy(note.at[far], notes.at[me.place], n_send, n_recv, (me.group, far)))
    notes[me.place] = note[me.place]
    lax.fori_loop(0, 2, slot, 0)
    wait_all(notes, n_send, n_recv)
    rows_in = notes.shape[1]
    step = 512
    for at_col in range(0, emb.shape[1], step):
        cols = slice(at_col, at_col + step)
        product = jnp.dot(notes[...].reshape(parts * rows_in, 128), emb[:, cols], preferred_element_type=jnp.float32)
        part[:, :, cols] = product.reshape(parts, rows_in, step)[:, :8]
    to_all(lambda far: copy(part.at[far], sums.at[me.place], m_send, m_recv, (me.group, far)))
    sums[me.place] = part[me.place]
    lax.fori_loop(2, chunks + DEPTH, slot, 0)
    local.wait()
    wait_all(sums, m_send, m_recv)
    mod[...] = jnp.sum(sums[...], axis=0)

    def finish(k, carry):
        for step, edge in ((1, me.z < DEPTH - 1), (-1, me.z > 0)):
            for s in range(DEPTH - 1):
                ok, z = below(s) if step > 0 else above(s)
                @pl.when(jnp.logical_and(ok, edge))
                def _():
                    z_copy(k, z, step, False).wait_send()
        for z in range(DEPTH):
            for turn in range(1, span):
                y_copy(k, z, turn, False).wait_send()
                x_copy(k, z, turn).wait_send()
            @pl.when(z != me.z)
            def _():
                thin_copy(k, z).wait_send()
        lane = full.at[pl.ds(0, parts // 2), at(k)]
        whole = copy(lane, lane, c_send.at[k], c_recv.at[k], me.device(core=1 - me.core))
        whole.wait_send()
        whole.wait_recv()
        return carry

    lax.fori_loop(0, chunks, finish, 0)


def gather_all(own, note, emb, replicas, parts, rows=80, lead=3):
    wide = emb.shape[1]
    total, width = own.shape
    chunks = total // rows
    span = parts // (2 * DEPTH)
    dma = lambda *shape: pltpu.SemaphoreType.DMA(shape)
    return pl.pallas_call(
        functools.partial(gather_kernel, replicas, parts, rows, lead),
        out_shape=[
            jax.ShapeDtypeStruct((parts, total, width), own.dtype),
            jax.ShapeDtypeStruct((8, wide), jnp.float32),
            jax.ShapeDtypeStruct(note.shape, note.dtype),
        ],
        in_specs=[pl.BlockSpec(memory_space=pl.ANY)] + [pl.BlockSpec(memory_space=pltpu.VMEM)] * 2,
        out_specs=[pl.BlockSpec(memory_space=pl.ANY)] + [pl.BlockSpec(memory_space=pltpu.VMEM)] * 2,
        scratch_shapes=[
            pltpu.VMEM((parts, 8, wide), jnp.float32),
            pltpu.VMEM((parts, 8, wide), jnp.float32),
            dma(), dma(), dma(), dma(),
            dma(chunks, DEPTH, 2), dma(chunks, DEPTH),
            dma(chunks, DEPTH, span - 1), dma(chunks, DEPTH, span - 1),
            dma(chunks, DEPTH), dma(chunks, DEPTH),
            dma(chunks, DEPTH, span - 1), dma(chunks, DEPTH, span - 1),
            dma(chunks), dma(chunks), pltpu.SemaphoreType.DMA,
        ],
        compiler_params=pltpu.CompilerParams(collective_id=0, has_side_effects=True, vmem_limit_bytes=40 << 20),
        name="gather_all",
    )(own, note, emb)


F32=jnp.float32


class Seat(Where):
    def bit(self, b):
        step = 1 << b
        group = self.group + step - 2 * step * lax.rem(self.group // step, 2)
        return (group, self.place)

    def meet(self, bits, everyone):
        sem = pltpu.get_barrier_semaphore()
        greet = lambda device: pl.semaphore_signal(sem, inc=1, device_id=device, device_id_type=MESH)
        if everyone:
            count = self.replicas * self.parts
            def one(i, carry):
                far = lax.rem(self.group * self.parts + self.place + i, count)
                greet((far // self.parts, lax.rem(far, self.parts)))
                return carry
            lax.fori_loop(1, count, one, 0)
            pl.semaphore_wait(sem, count - 1)
            return


def reduce_kernel(replicas, parts, rows, spans, lead, ring, nrc, lag, ngrad, *refs):
    grads, note, out, notes = refs[:ngrad], refs[ngrad], refs[ngrad + 1], refs[ngrad + 2]
    (hold, rc, xr, yr, zu, zd, fr, tb, l_sem, c_send, c_recv, x_send, x_recv, y_send, y_recv,
     u_send, u_recv, d_send, d_recv, f_send, f_recv, n_send, n_recv, free) = refs[ngrad + 3:]
    me = Seat(replicas, parts)
    span = me.span
    width = out.shape[1]
    chunks = out.shape[0] // rows
    side = me.side
    bits = replicas.bit_length() - 1
    apart, joint = 3 * width // 8, 5 * width // 8

    me.meet(bits, True)

    def copy(src, dst, send, recv, device):
        return pltpu.make_async_remote_copy(src_ref=src, dst_ref=dst, send_sem=send, recv_sem=recv, device_id=device, device_id_type=MESH)

    count = replicas * parts
    mine = me.group * parts + me.place

    def note_copy(far):
        return copy(note.at[lax.rem(far, parts)], notes.at[mine], n_send, n_recv, (far // parts, lax.rem(far, parts)))

    def send_note(i, carry):
        note_copy(lax.rem(mine + i, count)).start()
        return carry

    lax.fori_loop(1, count, send_note, 0)
    own_note = pltpu.make_async_copy(note.at[me.place], notes.at[mine], l_sem.at[ring])
    own_note.start()

    def core_copy(k, src):
        return copy(src, rc.at[lax.rem(k, nrc)], c_send.at[k], c_recv.at[lax.rem(k, nrc)], me.device(core=1 - me.core))

    def begin(k):
        @pl.when(k >= nrc)
        def _():
            pl.semaphore_wait(free, 1)
        for grad, (lo, hi) in zip(grads, spans):
            @pl.when(jnp.logical_and(k >= lo, k < hi))
            def _():
                at = pl.ds(pl.multiple_of((k - lo) * rows, 16), rows)
                slot = lax.rem(k, ring)
                pltpu.make_async_copy(grad.at[:, :, me.core, at, :], hold.at[slot], l_sem.at[slot]).start()
                core_copy(k, grad.at[:, :, 1 - me.core, at, :]).start()

    def x_copy(k, turn):
        slot = lax.rem(k, ring)
        cols = pl.ds(pl.multiple_of((1 - side) * joint, 128), apart)
        return copy(hold.at[slot, :, lax.rem(me.y + turn, span), :, cols], xr.at[k, turn - 1], x_send.at[k, turn - 1], x_recv.at[k, turn - 1], me.bit(0))

    def y_copy(k, turn):
        slot = lax.rem(k, ring)
        cols = pl.ds(pl.multiple_of(side * apart, 128), joint)
        return copy(hold.at[slot, :, lax.rem(me.y + turn, span), :, cols], yr.at[k, turn - 1], y_send.at[k, turn - 1], y_recv.at[k, turn - 1], me.device(y=lax.rem(me.y + turn, span)))

    def up_copy(k, z):
        slot = lax.rem(k, ring)
        return copy(hold.at[slot, z + 1 : DEPTH, me.y], zu.at[k, 0 : DEPTH - 1 - z], u_send.at[k], u_recv.at[k], me.device(z=me.z + 1))

    def down_copy(k, z):
        slot = lax.rem(k, ring)
        return copy(hold.at[slot, 0:z, me.y], zd.at[k, 0:z], d_send.at[k], d_recv.at[k], me.device(z=me.z - 1))

    def f_copy(k, b):
        slot = lax.rem(k, ring)
        src = hold.at[slot, me.z, me.y] if b == 0 else tb.at[b - 1, k]
        return copy(src, fr.at[b, k], f_send.at[b, k], f_recv.at[b, k], me.bit(b))

    def fold_core(k):
        slot = lax.rem(k, ring)
        here = hold.at[slot]
        pltpu.make_async_copy(here, here, l_sem.at[slot]).wait()
        core_copy(k, rc.at[lax.rem(k, nrc)]).wait_recv()
        hold[slot] = hold[slot] + rc[lax.rem(k, nrc)]
        @pl.when(k + nrc < chunks)
        def _():
            pl.semaphore_signal(free, inc=1, device_id=me.device(core=1 - me.core), device_id_type=MESH)
        for turn in range(1, span):
            x_copy(k, turn).start()

    def fold_x(k):
        slot = lax.rem(k, ring)
        for turn in range(1, span):
            x_copy(k, turn).wait_recv()
            y = lax.rem(me.y + turn, span)
            for s in range(2):
                @pl.when(side == s)
                def _():
                    cols = slice(0, apart) if s == 0 else slice(joint, width)
                    hold[slot, :, y, :, cols] = hold[slot, :, y, :, cols] + xr[k, turn - 1]
            y_copy(k, turn).start()

    def fold_y(k):
        slot = lax.rem(k, ring)
        for turn in range(1, span):
            y_copy(k, turn).wait_recv()
            for s in range(2):
                @pl.when(side == s)
                def _():
                    cols = slice(0, joint) if s == 0 else slice(apart, width)
                    hold[slot, :, me.y, :, cols] = hold[slot, :, me.y, :, cols] + yr[k, turn - 1]

    def hop(k, h):
        slot = lax.rem(k, ring)
        @pl.when(me.z == h)
        def _():
            if h > 0:
                up_copy(k, h - 1).wait_recv()
                hold[slot, h:, me.y] = hold[slot, h:, me.y] + zu[k, 0 : DEPTH - h]
            if h < DEPTH - 1:
                up_copy(k, h).start()
        z = DEPTH - 1 - h
        @pl.when(me.z == z)
        def _():
            if h > 0:
                down_copy(k, z + 1).wait_recv()
                hold[slot, : z + 1, me.y] = hold[slot, : z + 1, me.y] + zd[k, 0 : z + 1]
            if h < DEPTH - 1:
                down_copy(k, z).start()

    def finish(k, b):
        slot = lax.rem(k, ring)
        f_copy(k, b).wait_recv()
        before = hold[slot, me.z, me.y] if b == 0 else tb[b - 1, k]
        total = before.astype(F32) + fr[b, k].astype(F32)
        if b == bits - 1:
            out[pl.ds(pl.multiple_of(k * rows, 16), rows), :] = total
        else:
            tb[b, k] = total.astype(BF16)
            f_copy(k, b + 1).start()

    def retire(k):
        core_copy(k, rc.at[0]).wait_send()
        for turn in range(1, span):
            x_copy(k, turn).wait_send()
            y_copy(k, turn).wait_send()
        for z in range(DEPTH):
            @pl.when(me.z == z)
            def _():
                if z < DEPTH - 1:
                    up_copy(k, z).wait_send()
                if z > 0:
                    down_copy(k, z).wait_send()
        for b in range(bits):
            f_copy(k, b).wait_send()

    for k in range(lead):
        begin(jnp.int32(k))

    first_f = (2 + DEPTH) * lag

    def slot_work(t, carry):
        def stage(delay, work):
            k = t - delay
            @pl.when(jnp.logical_and(k >= 0, k < chunks))
            def _():
                work(k)
        for h in range(DEPTH - 1, 0, -1):
            stage((2 + h) * lag, functools.partial(hop, h=h))
        stage((1 + DEPTH) * lag, lambda k: f_copy(k, 0).start())
        def pair(k):
            fold_y(k)
            hop(k, 0)
        stage(2 * lag, pair)
        stage(lag, fold_x)
        stage(0, fold_core)
        for b in range(bits):
            stage(first_f + b * lag, functools.partial(finish, b=b))
        stage(first_f + bits * lag, retire)
        @pl.when(t + lead < chunks)
        def _():
            begin(t + lead)
        return carry

    lax.fori_loop(0, chunks + first_f + bits * lag + 1, slot_work, 0)
    own_note.wait()
    others = notes.at[pl.ds(0, count - 1)]
    every = copy(others, others, n_send, n_recv, me.device(core=1 - me.core))
    every.wait_send()
    every.wait_recv()


def reduce_all(grads, note, replicas, parts, rows, lead=2, nrc=3, lag=2):
    span = parts // (2 * DEPTH)
    width = grads[0].shape[1]
    spans, at = [], 0
    views = []
    for grad in grads:
        size = grad.shape[0] // parts
        spans.append((at // rows, (at + size) // rows))
        at += size
        views.append(grad.reshape(DEPTH, span, 2, size, width))
    total = at
    chunks = total // rows
    bits = replicas.bit_length() - 1
    ring = lead + (2 + DEPTH + bits) * lag + 2
    dma = lambda *shape: pltpu.SemaphoreType.DMA(shape)
    vm = lambda *shape: pltpu.VMEM(shape, BF16)
    return pl.pallas_call(
        functools.partial(reduce_kernel, replicas, parts, rows, spans, lead, ring, nrc, lag, len(grads)),
        out_shape=[jax.ShapeDtypeStruct((total, width), F32), jax.ShapeDtypeStruct((replicas * parts,) + note.shape[1:], note.dtype)],
        in_specs=[pl.BlockSpec(memory_space=pl.ANY)] * (len(grads) + 1),
        out_specs=[pl.BlockSpec(memory_space=pltpu.VMEM), pl.BlockSpec(memory_space=pl.ANY)],
        scratch_shapes=[
            vm(ring, DEPTH, span, rows, width),
            vm(nrc, DEPTH, span, rows, width),
            vm(chunks, span - 1, DEPTH, rows, 3 * width // 8),
            vm(chunks, span - 1, DEPTH, rows, 5 * width // 8),
            vm(chunks, DEPTH - 1, rows, width),
            vm(chunks, DEPTH - 1, rows, width),
            vm(bits, chunks, rows, width),
            vm(max(bits - 1, 1), chunks if bits > 1 else 1, rows, width),
            dma(ring + 1),
            dma(chunks), dma(nrc),
            dma(chunks, span - 1), dma(chunks, span - 1),
            dma(chunks, span - 1), dma(chunks, span - 1),
            dma(chunks), dma(chunks), dma(chunks), dma(chunks),
            dma(bits, chunks), dma(bits, chunks),
            pltpu.SemaphoreType.DMA, pltpu.SemaphoreType.DMA,
            pltpu.SemaphoreType.REGULAR,
        ],
        compiler_params=pltpu.CompilerParams(collective_id=1, has_side_effects=True, vmem_limit_bytes=60 << 20),
        name="reduce_all",
    )(*views, note)


HEADS = 8
HEAD = 64
GROUPS = 32
UNIT = 4
SHAPES = ((4 * UNIT, 4 * UNIT), (3 * UNIT, 5 * UNIT), (5 * UNIT, 3 * UNIT))
SIZES = tuple(height * breadth for height, breadth in SHAPES)
STARTS = (0, SIZES[0], SIZES[0] + SIZES[1])


def dot(left, right, dims=((1,), (0,))):
    return lax.dot_general(left, right, (dims, ((), ())), preferred_element_type=F32)


def images(rows):
    return [rows[start : start + size] for start, size in zip(STARTS, SIZES)]


def group_mean(column_sums, count):
    channels = column_sums.shape[-1]
    width = channels // GROUPS
    totals = jnp.sum(column_sums.reshape(GROUPS, width), axis=1, keepdims=True) / (count * width)
    return jnp.broadcast_to(totals, (GROUPS, width)).reshape(1, channels)


def normalise(rows):
    count = rows.shape[0]
    centered = rows - group_mean(jnp.sum(rows, axis=0), count)
    spread = group_mean(jnp.sum(jnp.square(centered), axis=0), count)
    inverse = lax.rsqrt(spread + 1e-05)
    return centered * inverse, inverse


def norm_back(grad, hat, inverse, factor):
    count = grad.shape[0]
    plain = jnp.sum(grad, axis=0)
    crossed = jnp.sum(grad * hat, axis=0)
    mean_plain = group_mean(plain * factor, count)
    mean_crossed = group_mean(crossed * factor, count)
    return inverse * (grad * factor[None, :] - mean_plain - hat * mean_crossed), plain, crossed


def silu_slope(value):
    gate = jax.nn.sigmoid(value)
    return gate * (1.0 + value * (1.0 - gate))


def patches(rows, flip=False):
    channels = rows.shape[-1]
    parts = []
    for (height, breadth), picture in zip(SHAPES, images(rows)):
        padded = jnp.pad(picture.reshape(height, breadth, channels), ((1, 1), (1, 1), (0, 0)))
        windows = [
            padded[down : down + height, across : across + breadth]
            for down in range(3)
            for across in range(3)
        ]
        if flip:
            windows = windows[::-1]
        parts.append(jnp.concatenate(windows, axis=-1).reshape(height * breadth, 9 * channels))
    return jnp.concatenate(parts, 0)


TEXT_PAD = 128


def attention_kernel(q_ref, k_ref, v_ref, tk_ref, tv_ref, mask_ref, go_ref, o_ref, dq_ref, dk_ref, dv_ref, dtk_ref, dtv_ref):
    lane = lax.broadcasted_iota(jnp.int32, (1, 2 * HEAD), 1)
    for image in range(3):
        rows = pl.ds(STARTS[image], SIZES[image])
        size = SIZES[image]
        q, k, v, go = q_ref[rows, :], k_ref[rows, :], v_ref[rows, :], go_ref[rows, :]
        tk, tv = tk_ref[image], tv_ref[image]
        mask = mask_ref[image : image + 1, :]
        results = []
        for head in range(2):
            mine = (lane >= HEAD) if head else (lane < HEAD)
            qh = jnp.where(mine, q, jnp.zeros_like(q))
            gh = jnp.where(mine, go, jnp.zeros_like(go))
            scale = HEAD ** -0.5
            nt = ((1,), (1,))
            tn = ((0,), (0,))
            sp = dot(qh, k, nt) * scale
            st = dot(qh, tk, nt) * scale
            st = jnp.where(mask == 1, st, jnp.where(mask == 0, -1000000000.0, -jnp.inf))
            peak = jnp.maximum(
                jnp.max(sp, axis=1, keepdims=True), jnp.max(st, axis=1, keepdims=True)
            )
            ep, et = jnp.exp(sp - peak), jnp.exp(st - peak)
            total = jnp.sum(ep, axis=1, keepdims=True) + jnp.sum(et, axis=1, keepdims=True)
            inv = 1.0 / total
            pp, pt = ep * inv, et * inv
            ppl, ptl = pp.astype(BF16), pt.astype(BF16)
            out = dot(ppl, v) + dot(ptl, tv)
            dv = dot(ppl, go, tn)
            dtv = dot(ptl, go, tn)
            dpp = dot(gh, v, nt)
            dpt = dot(gh, tv, nt)
            inner = jnp.sum(dpp * pp, axis=1, keepdims=True) + jnp.sum(
                dpt * pt, axis=1, keepdims=True
            )
            dsp = (pp * (dpp - inner) * scale).astype(BF16)
            dst = (pt * (dpt - inner) * scale).astype(BF16)
            dq = dot(dsp, k) + dot(dst, tk)
            dk = dot(dsp, q, tn)
            dtk = dot(dst, q, tn)
            results.append((out, dq, dk, dv, dtk, dtv))
        first, second = results
        low = lane < HEAD
        merged = [jnp.where(low, a, b).astype(BF16) for a, b in zip(first, second)]
        o_ref[rows, :] = merged[0]
        dq_ref[rows, :] = merged[1]
        dk_ref[rows, :] = merged[2]
        dv_ref[rows, :] = merged[3]
        dtk_ref[image] = merged[4]
        dtv_ref[image] = merged[5]


def attention(triple, text_pair, mask, grad_attended):
    rows, inner = triple.shape[0], triple.shape[1] // 3
    pairs = inner // (2 * HEAD)
    col = lambda shift: pl.BlockSpec((rows, 2 * HEAD), lambda h: (0, h + shift * pairs))
    txt = lambda shift: pl.BlockSpec((3, TEXT_PAD, 2 * HEAD), lambda h: (0, 0, h + shift * pairs))
    wide = jax.ShapeDtypeStruct((rows, inner), BF16)
    wide_text = jax.ShapeDtypeStruct((3, TEXT_PAD, inner), BF16)
    return pl.pallas_call(
        attention_kernel,
        grid=(pairs,),
        in_specs=[
            col(0),
            col(1),
            col(2),
            txt(0),
            txt(1),
            pl.BlockSpec((3, TEXT_PAD), lambda h: (0, 0)),
            col(0),
        ],
        out_specs=[col(0)] * 4 + [txt(0)] * 2,
        out_shape=[wide] * 4 + [wide_text] * 2,
        compiler_params=pltpu.CompilerParams(vmem_limit_bytes=40 << 20),
    )(triple, triple, triple, text_pair, text_pair, mask, grad_attended)


def body(
    pixels,
    embedding,
    text_states,
    text_mask,
    occupancy,
    cotangent,
    in_gain,
    in_shift,
    conv_first,
    first_bias,
    emb_weight,
    emb_bias,
    mid_gain,
    mid_shift,
    conv_second,
    second_bias,
    skip_weight,
    skip_bias,
    attn_gain,
    attn_shift,
    attend_weight,
    text_weight,
    out_weight,
    out_bias,
):
    place = lax.axis_index("fsdp")
    group = lax.axis_index("dp")
    parts = lax.axis_size("fsdp")
    replicas = lax.axis_size("dp")
    depth = emb_weight.shape[0]
    images_here = embedding.shape[0]
    emb_act = jax.nn.silu(embedding.astype(F32)).astype(BF16)
    emb_cut = emb_act.reshape(images_here, parts, depth).transpose(1, 0, 2)
    emb_cut = jnp.pad(emb_cut, ((0, 0), (0, 0), (0, 128 - depth)))

    vectors = (in_gain, in_shift, first_bias, emb_bias, mid_gain, mid_shift, second_bias, skip_bias, attn_gain, attn_shift, out_bias)
    flat = jnp.concatenate(vectors)
    room = 16 - images_here
    flat = jnp.pad(flat, (0, room * 128 - flat.shape[0])).reshape(1, room, 128)
    note = jnp.concatenate([emb_cut, jnp.broadcast_to(flat, (parts, room, 128))], 1)
    small = jnp.concatenate([skip_weight, out_weight, attend_weight.reshape(-1, skip_weight.shape[1])], 0)
    own = jnp.concatenate([conv_first, conv_second, text_weight, small], 0)
    full, modulation, notes = gather_all(own, note, jnp.pad(emb_weight, ((0, 128 - depth), (0, 0))), replicas, parts)
    packed = notes[:, images_here:].reshape(parts, -1).astype(F32)
    whole = []
    at = 0
    for vector in vectors:
        whole.append(packed[:, at : at + vector.shape[0]].reshape(-1))
        at += vector.shape[0]
    (in_gain, in_shift, first_bias, emb_bias, mid_gain, mid_shift, second_bias, skip_bias, attn_gain, attn_shift, out_bias) = whole
    modulation = modulation[:images_here] + emb_bias

    cuts = []
    at = 0
    for part in (conv_first, conv_second, text_weight, skip_weight, out_weight):
        size = part.shape[0]
        cuts.append(full[:, at : at + size].reshape(parts * size, -1))
        at += size
    attend_width = attend_weight.shape[1]
    attend_weight = full[:, at:].reshape(-1, attend_width)
    conv_first, conv_second, text_weight, skip_weight, out_weight = cuts
    channels = conv_first.shape[1]
    inner = out_weight.shape[0]
    scale, shift = modulation[:, :channels], modulation[:, channels:]

    pixel_hat = [normalise(part.astype(F32)) for part in images(pixels)]
    first_pre = [hat * in_gain + in_shift for hat, _ in pixel_hat]
    first_act = jnp.concatenate([jax.nn.silu(part) for part in first_pre], 0).astype(BF16)
    first_patches = patches(first_act)
    first_conv = dot(first_patches, conv_first) + first_bias
    mid_hat = [normalise(part) for part in images(first_conv)]
    mid_pre = [
        (hat * mid_gain + mid_shift) * (1.0 + scale[i]) + shift[i]
        for i, (hat, _) in enumerate(mid_hat)
    ]
    second_act = jnp.concatenate([jax.nn.silu(part) for part in mid_pre], 0).astype(BF16)
    second_patches = patches(second_act)
    residual = dot(pixels, skip_weight) + dot(second_patches, conv_second) + (skip_bias + second_bias)
    attn_hat = [normalise(part) for part in images(residual)]
    normed = jnp.concatenate([hat * attn_gain + attn_shift for hat, _ in attn_hat], 0).astype(BF16)
    triple = dot(normed, attend_weight).astype(BF16)
    text_len = text_states.shape[1]
    text_rows = text_states.reshape(3 * text_len, -1)
    text_pair = dot(text_rows, text_weight).astype(BF16).reshape(3, text_len, -1)
    text_pair = jnp.pad(text_pair, ((0, 0), (0, TEXT_PAD - text_len), (0, 0)))
    mask = jnp.pad(
        (text_mask > 0).astype(jnp.int32), ((0, 0), (0, TEXT_PAD - text_len)), constant_values=2
    )
    present = jnp.concatenate(
        [jnp.broadcast_to(occupancy[0, i].astype(F32), (SIZES[i], 1)) for i in range(3)], 0
    )
    grad_out = cotangent.astype(F32) * present
    grad_low = grad_out.astype(BF16)
    grad_attended = dot(grad_low, out_weight, ((1,), (1,))).astype(BF16)
    attended, dq, dk, dv, dtk, dtv = attention(triple, text_pair, mask, grad_attended)
    block_output = (present * (residual + (dot(attended, out_weight) + out_bias))).astype(BF16)

    tn = ((0,), (0,))
    nt = ((1,), (1,))
    grad_out_bias = jnp.sum(grad_out, axis=0)
    grad_out_weight = dot(attended, grad_low, tn)
    grad_triple = jnp.concatenate([dq, dk, dv], 1)
    grad_text = jnp.concatenate([dtk, dtv], 2)[:, :text_len].reshape(3 * text_len, -1)
    grad_attend_weight = dot(normed, grad_triple, tn)
    grad_text_weight = dot(text_rows, grad_text, tn)
    grad_normed = dot(grad_triple, attend_weight, nt)
    backs = [
        norm_back(part, hat, inverse, attn_gain)
        for part, (hat, inverse) in zip(images(grad_normed), attn_hat)
    ]
    grad_attn_shift = sum(back[1] for back in backs)
    grad_attn_gain = sum(back[2] for back in backs)
    grad_residual = jnp.concatenate([back[0] for back in backs], 0) + grad_out
    grad_second_bias = jnp.sum(grad_residual, axis=0)
    res_low = grad_residual.astype(BF16)
    grad_skip_weight = dot(pixels, res_low, tn)
    grad_conv_second = dot(second_patches, res_low, tn)
    res_patches = patches(res_low, flip=True).reshape(-1, 9, channels)
    grad_second_act = lax.dot_general(
        res_patches,
        conv_second.reshape(9, channels, channels),
        (((1, 2), (0, 2)), ((), ())),
        preferred_element_type=F32,
    )
    backs = []
    grad_mod = []
    for i, part in enumerate(images(grad_second_act)):
        hat, inverse = mid_hat[i]
        grad_pre = part * silu_slope(mid_pre[i])
        factor = 1.0 + scale[i]
        rows, plain, crossed = norm_back(grad_pre, hat, inverse, factor * mid_gain)
        grad_mod.append(jnp.concatenate([crossed * mid_gain + plain * mid_shift, plain]))
        backs.append((rows, plain * factor, crossed * factor))
    grad_mid_shift = sum(back[1] for back in backs)
    grad_mid_gain = sum(back[2] for back in backs)
    grad_first_conv = jnp.concatenate([back[0] for back in backs], 0)
    grad_first_bias = jnp.sum(grad_first_conv, axis=0)
    conv_low = grad_first_conv.astype(BF16)
    grad_conv_first = dot(first_patches, conv_low, tn)
    first_width = pixels.shape[1]
    conv_patches = patches(conv_low, flip=True).reshape(-1, 9, channels)
    grad_first_act = lax.dot_general(
        conv_patches,
        conv_first.reshape(9, first_width, channels),
        (((1, 2), (0, 2)), ((), ())),
        preferred_element_type=F32,
    )
    backs = [
        norm_back(part * silu_slope(pre), hat, inverse, in_gain)
        for part, pre, (hat, inverse) in zip(images(grad_first_act), first_pre, pixel_hat)
    ]
    grad_in_shift = sum(back[1] for back in backs)
    grad_in_gain = sum(back[2] for back in backs)
    grad_pixels = jnp.concatenate([back[0] for back in backs], 0) + dot(res_low, skip_weight, nt)

    small = (grad_in_gain, grad_in_shift, grad_first_bias, grad_mid_gain, grad_mid_shift, grad_second_bias, grad_attn_gain, grad_attn_shift, grad_out_bias)
    cut = jnp.concatenate([vector.reshape(parts, -1) for vector in small], 1)
    mod_rows = jnp.stack(grad_mod).reshape(1, -1, 128)
    mod_count = mod_rows.shape[1]
    room = 64 - mod_count - images_here
    cut = jnp.pad(cut, ((0, 0), (0, room * 128 - cut.shape[1]))).reshape(parts, room, 128)
    note = jnp.concatenate(
        [jnp.broadcast_to(mod_rows, (parts,) + mod_rows.shape[1:]).astype(BF16), emb_cut, cut.astype(BF16)], 1
    )
    pack = lambda part: part.reshape(parts, -1, channels)
    grad_small = jnp.concatenate(
        [pack(grad_skip_weight), pack(grad_out_weight), pack(grad_attend_weight)], 1
    ).astype(BF16).reshape(-1, channels)
    owned, notes = reduce_all(
        [grad_conv_first.astype(BF16), grad_conv_second.astype(BF16), grad_text_weight.astype(BF16), grad_small],
        note, replicas, parts, 512 // parts,
    )
    at = 0
    cuts = []
    for size in (conv_first.shape[0], conv_second.shape[0], text_weight.shape[0], skip_weight.shape[0], out_weight.shape[0]):
        cuts.append(owned[at : at + size // parts])
        at += size // parts
    grad_conv_first, grad_conv_second, grad_text_weight, grad_skip_weight, grad_out_weight = cuts
    grad_attend_weight = owned[at:].reshape(-1, attend_width)
    mod_rows = notes[:, :mod_count].reshape(-1, 2 * channels)
    all_act = notes[:, mod_count : mod_count + images_here, :depth].reshape(-1, depth)
    grad_emb_weight = dot(all_act, mod_rows, tn)
    grad_emb_bias = jnp.sum(mod_rows.astype(F32), axis=0)
    grad_emb_bias = lax.dynamic_slice_in_dim(grad_emb_bias, place * depth, depth, 0)
    packed = jnp.sum(notes[:, mod_count + images_here :].astype(F32), axis=0).reshape(-1)
    owned = []
    at = 0
    for vector in small:
        size = vector.shape[0] // parts
        owned.append(packed[at : at + size])
        at += size
    (grad_in_gain, grad_in_shift, grad_first_bias, grad_mid_gain, grad_mid_shift, grad_second_bias, grad_attn_gain, grad_attn_shift, grad_out_bias) = owned

    return (
        block_output,
        grad_pixels,
        grad_in_gain,
        grad_in_shift,
        grad_conv_first,
        grad_first_bias,
        grad_emb_weight,
        grad_emb_bias,
        grad_mid_gain,
        grad_mid_shift,
        grad_conv_second,
        grad_second_bias,
        grad_skip_weight,
        grad_second_bias,
        grad_attn_gain,
        grad_attn_shift,
        grad_attend_weight,
        grad_text_weight,
        grad_out_weight,
        grad_out_bias,
    )


def solution(mesh):
    rows = P(("dp", "fsdp"), None)
    vector = P("fsdp")
    matrix = P("fsdp", None)
    weights = (vector, vector, matrix, vector, matrix, vector, vector, vector, matrix, vector, matrix, vector, vector, vector, matrix, matrix, matrix, vector)
    return jax.shard_map(
        body,
        mesh=mesh,
        in_specs=(rows, rows, P(("dp", "fsdp"), None, None), rows, rows, rows) + weights,
        out_specs=(rows, rows) + weights,
        check_vma=False,
    )
```

time: 1550 us -> 1060 us (0.68)
  waiting for transfers between devices: 579 us -> 0 us
  Pallas kernels: 0 us -> 426 us
  matrix products: 362 us -> 141 us
  blocking collectives: 146 us -> 0 us
  local copies, waits for them, and re-layouts: 325 us -> 396 us
  other arithmetic: 101 us -> 76.2 us
  between operations: 23.1 us -> 5.45 us
    pallas_call x0 -> x3, Pallas kernels: none -> 426 us  [the longest x1 204 us: reduce_all(): pl.pallas_call(functools.partial(reduce_kernel, replicas, parts, rows, sp...]
    reduce_scatter x6 -> x0, waiting for transfers between devices: 391 us -> none  [body(): lax.psum_scatter(for_sending(grad_sums), 'fsdp', scatter_dimension=0, til...]
    dot_general x72 -> x18, matrix products: 362 us -> 141 us  [the longest x16 107 us: dot(): lax.dot_general(left, right, (dims, ((), ())), preferred_element_type=F32)]
    all_gather x7 -> x0, waiting for transfers between devices: 183 us -> none  [the longest x1 71.2 us: body(): lax.all_gather(shards[2], 'fsdp', axis=0, tiled=True)]
    unnamed x2 -> x0, blocking collectives: 123 us -> none
    concatenate x38 -> x76, local copies, waits for them, and re-layouts: 49.3 us -> 119 us  [patches(): jnp.concatenate(windows, axis=-1).reshape(height * breadth, 9 * channels)]
    concatenate x9 -> x10, local copies, waits for them, and re-layouts: 5.61 us -> 50.6 us  [the longest x2 36.7 us: patches(): return jnp.concatenate(parts, 0)]
    convert_element_type x42 -> x2, other arithmetic: 37.9 us -> 0.7 us  [the longest x1 0.69 us: body(): (text_mask > 0).astype(jnp.int32)]
  transfers between devices with their start and end apart: 15 -> 0, of which waited for: 8 -> 0; matrix products, arithmetic and copies ran while one was open for 40% -> 0% of each run, Pallas kernels for 0% -> 0%
where the time goes in v1:
time: 1060 us; the launch traced here: 1050 us
  Pallas kernels  426 us (40%)
  local copies, waits for them, and re-layouts  396 us (37%)
  matrix products  141 us (13%)
  other arithmetic  76.2 us (7%)
    pallas_call x1, Pallas kernels, reduce_all(): pl.pallas_call(functools.partial(reduce_kernel, replicas, parts, rows, sp...  204 us
    pallas_call x1, Pallas kernels, gather_all(): pl.pallas_call(functools.partial(gather_kernel, replicas, parts, rows, le...  197 us
    concatenate x76, local copies, waits for them, and re-layouts, patches(): jnp.concatenate(windows, axis=-1).reshape(height * breadth, 9 * channels)  119 us
    dot_general x16, matrix products, dot(): lax.dot_general(left, right, (dims, ((), ())), preferred_element_type=F32)  107 us
    unnamed x371, local copies, waits for them, and re-layouts  84.6 us
    slice x4, local copies, waits for them, and re-layouts, body(): cuts.append(full[:, at:at + size].reshape(parts * size, -1))  38.2 us
    concatenate x2, local copies, waits for them, and re-layouts, patches(): return jnp.concatenate(parts, 0)  36.7 us
    slice x12, local copies, waits for them, and re-layouts, patches(): padded[down:down + height, across:across + breadth]  32.2 us

profile of v1, /device:TPU:0, one launch (start us, length us, event | category | flops | bytes accessed | tf_op | source)
XLA Modules:
  0.0 1045.1 jit_solution(3482863738031376786)
XLA Ops:
  4.8 7.4 concatenate.320
  20.9 3.3 reshape.856
  25.6 196.8 %gather_all.1 = (bf16[16,1280,1024]{2,1,0:T(8,128)(2,1)}, f32[8,2048]{1,0:T(8,128)S(1)}, bf16[16,16,128]{2,1,0:T(8,128)(2,1)S(1)}) custom-call(bf16[1280,1024]{1,0:T(8,128)(2,1)S(1)} %constant_dynamic-update-slice_fusion.own, bf16[16,16,128]{2,1,0:T(8,128)(2,1)S(1)} %pad_maximum_fusion.19.note, bf16[128,2048]{1,0:T(8,128)(2,1)S(1)} %copy-done), custom_call_target="tpu_custom_call" | custom-call | tf_op jit(solution)/shard_map/gather_all/pallas_call | solution.py:229
  246.0 2.7 fusion.113
  284.6 2.6 fusion.123
  287.2 4.0 slice.629
  291.1 6.2 reshape.854
  297.4 8.1 slice.630
  305.4 5.6 fusion.12
  311.2 8.8 slice.579
  320.0 18.6 %slice.621 = bf16[16,576,1024]{2,1,0:T(8,128)(2,1)} slice(bf16[16,1280,1024]{2,1,0:T(8,128)(2,1)} %get-tuple-element.31), slice={[0:16], [288:864], [0:1024]} | slice | bytes 37748736 | tf_op jit(solution)/shard_map/slice | solution.py:702
  338.6 9.5 fusion.6
  355.0 2.4 multiply_convert_fusion.1
  357.5 3.0 multiply_convert_fusion.3
  363.4 5.4 pad_slice_fusion.16
  368.8 2.5 pad_slice_fusion.48
  399.8 3.0 pad_slice_fusion.72
  423.9 3.4 constant_dynamic-update-slice_fusion.37
  427.9 27.6 %fusion.2 = f32[736,1024]{1,0:T(8,128)S(1)} fusion(f32[1024,736]{0,1:T(8,128)S(1)} %copy-done.9, bf16[9216,1024]{1,0:T(8,128)(2,1)} %bitcast.123, bf16[240,9216]{1,0:T(8,128)(2,1)S(1)} %constant_dynamic-update-slice_fusion.51, bf16[240,9216]{1,0:T(8,128)(2,1)} %constant_dynamic-update-slice_fusion.42, ...), kind=kOutput, calls=%fused_computation.14 | convolution fusion | flops 13933740032 | bytes 38473728 | tf_op jit(solution)/shard_map/dot_general | solution.py:513
  465.9 2.5 convolution_convert_fusion.3.q_ref.k_ref.v_ref
  468.4 24.4 %shard_map.383 = (bf16[736,512]{1,0:T(8,128)(2,1)S(1)}, bf16[736,512]{1,0:T(8,128)(2,1)S(1)}, bf16[736,512]{1,0:T(8,128)(2,1)S(1)}, bf16[736,512]{1,0:T(8,128)(2...) custom-call(bf16[736,1536]{1,0:T(8,128)(2,1)S(1)} %convolution_convert_fusion.3.q_ref.k_ref.v_ref, ...), custom_call_target="tpu_custom_call" | custom-call | tf_op jit(solution)/shard_map/pallas_call | solution.py:627
  497.2 4.2 fusion.121
  501.4 4.0 convolution_convert_fusion.2
  505.4 6.3 concatenate.442
  513.6 2.6 multiply_reduce_fusion.7
  531.0 2.8 pad_maximum_fusion.6.refs_3_
  536.1 2.5 pad_slice_fusion.40
  561.5 5.1 pad_slice_fusion.64
  595.2 8.1 pad_maximum_fusion.1
  603.2 18.4 %copy.52 = bf16[736,9216]{0,1:T(8,128)(2,1)} copy(bf16[736,9216]{1,0:T(8,128)(2,1)} %pad_maximum_fusion.1) | data formatting | bytes 27131904 | tf_op jit(solution)/shard_map/concatenate | solution.py:562
  621.7 20.4 %convolution_bitcast_fusion = f32[736,1024]{1,0:T(8,128)S(1)} fusion(bf16[736,9,1024]{0,2,1:T(8,128)(2,1)} %bitcast.126, bf16[9,1024,1024]{2,1,0:T(8,128)(2,1)} %bitcast.124), kind=kOutput, calls=%fused_computation.20 | convolution fusion | flops 13891534848 | bytes 35454976 | tf_op jit(solution)/shard_map/dot_general | solution.py:764
  643.9 2.4 multiply_reduce_fusion.5
  648.2 3.6 fusion.90
  652.1 2.7 fusion.87
  658.8 12.5 %convolution_convert_fusion.1 = bf16[4608,1024]{1,0:T(8,128)(2,1)} fusion(bf16[240,4608]{1,0:T(8,128)(2,1)} %copy-done.129, bf16[240,4608]{1,0:T(8,128)(2,1)} %constant_dynamic-update-slice_fusion.15, bf16[256,4608]{1,0:T(8,128)(2,1)} %constant_dynamic-update-slice_fusion.6, bf16[240,1024]{1,0:T(8,128)(2,1)} %get-tuple-element.116, ...), kind=kOutput, calls=%fused_computation.5 | convolution fusion | flops 6975356928 | bytes 17727488 | tf_op jit(solution)/shard_map/dot_general | solution.py:513
  671.3 2.5 pad_slice_fusion.32
  704.6 2.8 pad_slice_fusion.56
  730.7 8.1 pad_maximum_fusion.2
  738.8 18.4 %copy.54 = bf16[736,9216]{0,1:T(8,128)(2,1)} copy(bf16[736,9216]{1,0:T(8,128)(2,1)} %pad_maximum_fusion.2) | data formatting | bytes 27131904 | tf_op jit(solution)/shard_map/concatenate | solution.py:562
  757.2 13.6 %convolution_bitcast_fusion.1 = f32[736,512]{1,0:T(8,128)S(1)} fusion(bf16[736,9,1024]{0,2,1:T(8,128)(2,1)} %bitcast.127, bf16[9,512,1024]{2,1,0:T(8,128)(2,1)} %bitcast.129), kind=kOutput, calls=%fused_computation.31 | convolution fusion | flops 6945767424 | bytes 24510464 | tf_op jit(solution)/shard_map/dot_general | solution.py:787
  775.3 2.4 fusion.79
  779.1 3.6 maximum_add_fusion.1
  783.5 20.8 %convolution_convert_fusion = bf16[9216,1024]{1,0:T(8,128)(2,1)} fusion(bf16[736,1024]{1,0:T(8,128)(2,1)S(1)} %get-tuple-element.113, bf16[240,9216]{1,0:T(8,128)(2,1)} %copy-done.111, bf16[240,9216]{1,0:T(8,128)(2,1)} %constant_dynamic-update-slice_fusion.42, bf16[256,9216]{1,0:T(8,128)(2,1)} %copy-done.110), kind=kOutput, calls=%fused_computation | convolution fusion | flops 13941669888 | bytes 33947648 | tf_op jit(solution)/shard_map/dot_general | solution.py:513
  804.4 5.6 fusion
  810.0 11.9 %copy.56 = bf16[4096,1024]{1,0:T(8,128)(2,1)} copy(bf16[4096,1024]{0,1:T(8,128)(2,1)} %fusion) | data formatting | bytes 16777216 | tf_op jit(solution)/shard_map/convert_element_type | solution.py:815
  821.9 204.3 %reduce_all.1 = (f32[1280,1024]{1,0:T(8,128)}, bf16[32,64,128]{2,1,0:T(8,128)(2,1)}) custom-call(bf16[4,2,2,288,1024]{4,3,2,1,0:T(8,128)(2,1)} %bitcast.128, bf16[4,2,2,576,1024]{4,3,2,1,0:T(8,128)(2,1)} %bitcast.125, bf16[4,2,2,256,1024]{4,3,2,1,0:T(8,128)(2,1)} %bitcast.122, bf16[4,2,2,160,1024]{4,3,2,1,0:T(8,128)(2,1)} %pad_maximum_fusion.6.refs_3_, ...), custom_call_target="tpu_custom_call" | custom-call | tf_op jit(solution)/shard_map/reduce_all/pallas_call | solution.py:475
  1038.3 2.4 slice.700
  1040.7 3.4 slice.706
  (747 shorter events, 296.4 us)
Async XLA Ops:
  0.7 23.6 %copy-start.70 = (bf16[576,1024]{1,0:T(8,128)(2,1)S(1)}, bf16[576,1024]{1,0:T(8,128)(2,1)}, u32[]{:S(2)}) copy-start(bf16[576,1024]{1,0:T(8,128)(2,1)} %param.38) | copy-start | bytes 3538948
  0.7 23.6 %copy-start.82 = (bf16[288,1024]{1,0:T(8,128)(2,1)S(1)}, bf16[288,1024]{1,0:T(8,128)(2,1)}, u32[]{:S(2)}) copy-start(bf16[288,1024]{1,0:T(8,128)(2,1)} %param.32) | copy-start | bytes 1769476
  15.0 265.7 %copy-start.91 = (f32[512]{0:T(512)}, f32[512]{0:T(512)S(1)}, u32[]{:S(2)}) copy-start(f32[512]{0:T(512)S(1)} %sub.225) | copy-start | bytes 6148
  16.5 264.3 %copy-start.112 = (f32[512]{0:T(512)}, f32[512]{0:T(512)S(1)}, u32[]{:S(2)}) copy-start(f32[512]{0:T(512)S(1)} %rsqrt.109) | copy-start | bytes 6148
  16.6 213.0 %copy-start.114 = (f32[512]{0:T(512)}, f32[512]{0:T(512)S(1)}, u32[]{:S(2)}) copy-start(f32[512]{0:T(512)S(1)} %sub.228) | copy-start | bytes 6148
  17.8 211.9 %copy-start.116 = (f32[512]{0:T(512)}, f32[512]{0:T(512)S(1)}, u32[]{:S(2)}) copy-start(f32[512]{0:T(512)S(1)} %sub.231) | copy-start | bytes 6148
  19.3 210.3 %copy-start.125 = (f32[512]{0:T(512)}, f32[512]{0:T(512)S(1)}, u32[]{:S(2)}) copy-start(f32[512]{0:T(512)S(1)} %rsqrt.111) | copy-start | bytes 6148
  19.7 210.0 %copy-start.127 = (f32[512]{0:T(512)}, f32[512]{0:T(512)S(1)}, u32[]{:S(2)}) copy-start(f32[512]{0:T(512)S(1)} %rsqrt.113) | copy-start | bytes 6148
  24.3 205.2 %copy-start.6 = (bf16[736,512]{1,0:T(8,128)(2,1)S(1)}, bf16[736,512]{1,0:T(8,128)(2,1)}, u32[]{:S(2)}) copy-start(bf16[736,512]{1,0:T(8,128)(2,1)} %param.24) | copy-start | bytes 2260996
  222.7 58.0 %copy-start.93 = (f32[512]{0:T(512)}, f32[512]{0:T(512)S(1)}, u32[]{:S(2)}) copy-start(f32[512]{0:T(512)S(1)} %add.460) | copy-start | bytes 6148
  222.9 57.9 %copy-start.85 = (f32[512]{0:T(512)}, f32[512]{0:T(512)S(1)}, u32[]{:S(2)}) copy-start(f32[512]{0:T(512)S(1)} %mul.653) | copy-start | bytes 6148
  225.4 132.0 %copy-start.106 = (f32[1,1024]{1,0:T(1,128)}, f32[1,1024]{1,0:T(1,128)S(1)}, u32[]{:S(2)}) copy-start(f32[1,1024]{1,0:T(1,128)S(1)} %get-tuple-element.242) | copy-start | bytes 12292
  225.4 132.0 %copy-start.108 = (f32[1,1024]{1,0:T(1,128)}, f32[1,1024]{1,0:T(1,128)S(1)}, u32[]{:S(2)}) copy-start(f32[1,1024]{1,0:T(1,128)S(1)} %get-tuple-element.244) | copy-start | bytes 12292
  225.5 132.0 %copy-start.118 = (f32[1,1024]{1,0:T(1,128)}, f32[1,1024]{1,0:T(1,128)S(1)}, u32[]{:S(2)}) copy-start(f32[1,1024]{1,0:T(1,128)S(1)} %get-tuple-element.241) | copy-start | bytes 12292
  225.5 132.0 %copy-start.120 = (f32[1,1024]{1,0:T(1,128)}, f32[1,1024]{1,0:T(1,128)S(1)}, u32[]{:S(2)}) copy-start(f32[1,1024]{1,0:T(1,128)S(1)} %get-tuple-element.243) | copy-start | bytes 12292
  263.3 16.8 %copy-start.76 = (bf16[16,16,512]{2,1,0:T(8,128)(2,1)S(1)}, bf16[16,16,512]{2,1,0:T(8,128)(2,1)}, u32[]{:S(2)}) copy-start(bf16[16,16,512]{2,1,0:T(8,128)(2,1)} %get-tuple-element.221) | copy-start | bytes 786436
  265.1 16.6 %copy-start.75 = (bf16[16,16,512]{2,1,0:T(8,128)(2,1)S(1)}, bf16[16,16,512]{2,1,0:T(8,128)(2,1)}, u32[]{:S(2)}) copy-start(bf16[16,16,512]{2,1,0:T(8,128)(2,1)} %get-tuple-element.222) | copy-start | bytes 786436
  266.1 16.3 %copy-start.74 = (bf16[16,16,512]{2,1,0:T(8,128)(2,1)S(1)}, bf16[16,16,512]{2,1,0:T(8,128)(2,1)}, u32[]{:S(2)}) copy-start(bf16[16,16,512]{2,1,0:T(8,128)(2,1)} %get-tuple-element.223) | copy-start | bytes 786436
  266.1 17.0 %copy-start.73 = (bf16[16,16,512]{2,1,0:T(8,128)(2,1)S(1)}, bf16[16,16,512]{2,1,0:T(8,128)(2,1)}, u32[]{:S(2)}) copy-start(bf16[16,16,512]{2,1,0:T(8,128)(2,1)} %get-tuple-element.224) | copy-start | bytes 786436
  266.1 17.7 %copy-start.72 = (bf16[16,16,512]{2,1,0:T(8,128)(2,1)S(1)}, bf16[16,16,512]{2,1,0:T(8,128)(2,1)}, u32[]{:S(2)}) copy-start(bf16[16,16,512]{2,1,0:T(8,128)(2,1)} %get-tuple-element.218) | copy-start | bytes 786436
  267.0 17.6 %copy-start.12 = (bf16[16,32,1024]{2,1,0:T(8,128)(2,1)S(1)}, bf16[16,32,1024]{2,1,0:T(8,128)(2,1)}, u32[]{:S(2)}) copy-start(bf16[16,32,1024]{2,1,0:T(8,128)(2,1)} %get-tuple-element.108) | copy-start | bytes 3145732
  320.0 18.6 %copy-start.8 = (bf16[16,288,1024]{2,1,0:T(8,128)(2,1)S(1)}, bf16[16,288,1024]{2,1,0:T(8,128)(2,1)}, u32[]{:S(2)}) copy-start(bf16[16,288,1024]{2,1,0:T(8,128)(2,1)} %slice.579) | copy-start | bytes 28311556
  320.0 18.6 %copy-start.130 = (bf16[240,4608]{1,0:T(8,128)(2,1)S(1)}, bf16[240,4608]{1,0:T(8,128)(2,1)}, u32[]{:S(2)}) copy-start(bf16[240,4608]{1,0:T(8,128)(2,1)} %copy-done.129) | copy-start | bytes 6635524
  354.6 14.2 %copy-start.102 = (f32[1024]{0:T(1024)}, f32[1024]{0:T(1024)S(1)}, u32[]{:S(2)}) copy-start(f32[1024]{0:T(1024)S(1)} %rsqrt.117) | copy-start | bytes 12292
  355.0 13.8 %copy-start.104 = (f32[1024]{0:T(1024)}, f32[1024]{0:T(1024)S(1)}, u32[]{:S(2)}) copy-start(f32[1024]{0:T(1024)S(1)} %rsqrt.119) | copy-start | bytes 12292
  427.9 27.6 %copy-start.110 = (bf16[256,9216]{1,0:T(8,128)(2,1)}, bf16[256,9216]{1,0:T(8,128)(2,1)S(1)}, u32[]{:S(2)}) copy-start(bf16[256,9216]{1,0:T(8,128)(2,1)S(1)} %constant_dynamic-update-slice_fusion.33) | copy-start | bytes 14155780
  468.4 24.5 %copy-start.4 = (f32[736,1024]{1,0:T(8,128)S(1)}, f32[736,1024]{1,0:T(8,128)}, u32[]{:S(2)}) copy-start(f32[736,1024]{1,0:T(8,128)} %copy-done.3) | copy-start | bytes 9043972
  468.4 24.5 %copy-start.78 = (bf16[16,32,1024]{2,1,0:T(8,128)(2,1)S(1)}, bf16[16,32,1024]{2,1,0:T(8,128)(2,1)}, u32[]{:S(2)}) copy-start(bf16[16,32,1024]{2,1,0:T(8,128)(2,1)} %copy-done.77) | copy-start | bytes 3145732
  621.6 20.5 %copy-start.2 = (f32[736,1024]{1,0:T(8,128)S(1)}, f32[736,1024]{1,0:T(8,128)}, u32[]{:S(2)}) copy-start(f32[736,1024]{1,0:T(8,128)} %copy-done.1) | copy-start | bytes 9043972
  621.6 22.2 %copy-start.88 = (f32[1024]{0:T(1024)S(1)}, f32[1024]{0:T(1024)}, u32[]{:S(2)}) copy-start(f32[1024]{0:T(1024)} %copy-done.87) | copy-start | bytes 12292
  621.6 22.2 %copy-start.90 = (f32[1024]{0:T(1024)S(1)}, f32[1024]{0:T(1024)}, u32[]{:S(2)}) copy-start(f32[1024]{0:T(1024)} %copy-done.89) | copy-start | bytes 12292
  621.6 22.2 %copy-start.103 = (f32[1024]{0:T(1024)S(1)}, f32[1024]{0:T(1024)}, u32[]{:S(2)}) copy-start(f32[1024]{0:T(1024)} %copy-done.102) | copy-start | bytes 12292
  621.6 22.2 %copy-start.105 = (f32[1024]{0:T(1024)S(1)}, f32[1024]{0:T(1024)}, u32[]{:S(2)}) copy-start(f32[1024]{0:T(1024)} %copy-done.104) | copy-start | bytes 12292
  621.6 22.2 %copy-start.107 = (f32[1,1024]{1,0:T(1,128)S(1)}, f32[1,1024]{1,0:T(1,128)}, u32[]{:S(2)}) copy-start(f32[1,1024]{1,0:T(1,128)} %copy-done.106) | copy-start | bytes 12292
  621.6 22.2 %copy-start.109 = (f32[1,1024]{1,0:T(1,128)S(1)}, f32[1,1024]{1,0:T(1,128)}, u32[]{:S(2)}) copy-start(f32[1,1024]{1,0:T(1,128)} %copy-done.108) | copy-start | bytes 12292
  621.6 22.2 %copy-start.119 = (f32[1,1024]{1,0:T(1,128)S(1)}, f32[1,1024]{1,0:T(1,128)}, u32[]{:S(2)}) copy-start(f32[1,1024]{1,0:T(1,128)} %copy-done.118) | copy-start | bytes 12292
  621.7 22.2 %copy-start.121 = (f32[1,1024]{1,0:T(1,128)S(1)}, f32[1,1024]{1,0:T(1,128)}, u32[]{:S(2)}) copy-start(f32[1,1024]{1,0:T(1,128)} %copy-done.120) | copy-start | bytes 12292
  757.2 13.7 %copy-start.86 = (f32[512]{0:T(512)S(1)}, f32[512]{0:T(512)}, u32[]{:S(2)}) copy-start(f32[512]{0:T(512)} %copy-done.85) | copy-start | bytes 6148
  757.2 13.7 %copy-start.92 = (f32[512]{0:T(512)S(1)}, f32[512]{0:T(512)}, u32[]{:S(2)}) copy-start(f32[512]{0:T(512)} %copy-done.91) | copy-start | bytes 6148
  757.2 13.7 %copy-start.94 = (f32[512]{0:T(512)S(1)}, f32[512]{0:T(512)}, u32[]{:S(2)}) copy-start(f32[512]{0:T(512)} %copy-done.93) | copy-start | bytes 6148
  757.2 13.7 %copy-start.113 = (f32[512]{0:T(512)S(1)}, f32[512]{0:T(512)}, u32[]{:S(2)}) copy-start(f32[512]{0:T(512)} %copy-done.112) | copy-start | bytes 6148
  757.2 14.8 %copy-start.115 = (f32[512]{0:T(512)S(1)}, f32[512]{0:T(512)}, u32[]{:S(2)}) copy-start(f32[512]{0:T(512)} %copy-done.114) | copy-start | bytes 6148
  757.2 14.8 %copy-start.117 = (f32[512]{0:T(512)S(1)}, f32[512]{0:T(512)}, u32[]{:S(2)}) copy-start(f32[512]{0:T(512)} %copy-done.116) | copy-start | bytes 6148
  757.2 14.8 %copy-start.126 = (f32[512]{0:T(512)S(1)}, f32[512]{0:T(512)}, u32[]{:S(2)}) copy-start(f32[512]{0:T(512)} %copy-done.125) | copy-start | bytes 6148
  757.2 14.8 %copy-start.128 = (f32[512]{0:T(512)S(1)}, f32[512]{0:T(512)}, u32[]{:S(2)}) copy-start(f32[512]{0:T(512)} %copy-done.127) | copy-start | bytes 6148
  757.2 17.0 %copy-start.95 = (f32[32,16]{1,0:T(8,128)S(1)}, f32[32,16]{1,0:T(8,128)}, u32[]{:S(2)}) copy-start(f32[32,16]{1,0:T(8,128)} %reshape.870) | copy-start | bytes 6148
  783.5 20.8 %copy-start.44 = (bf16[3,77,4096]{2,1,0:T(8,128)(2,1)S(1)}, bf16[3,77,4096]{2,1,0:T(8,128)(2,1)}, u32[]{:S(2)}) copy-start(bf16[3,77,4096]{2,1,0:T(8,128)(2,1)} %param.26) | copy-start | bytes 5677060
  1028.4 15.7 %copy-start.134 = (f32[64]{0:T(128)}, f32[64]{0:T(128)S(1)}, u32[]{:S(2)}) copy-start(f32[64]{0:T(128)S(1)} %get-tuple-element.302) | copy-start | bytes 772
  (87 other events, 485.0 us)

commit v2 on v1

--- a/solution.py
+++ b/solution.py
@@ -7,8 +7,291 @@
 from jax.experimental.pallas import tpu as pltpu
 from jax.sharding import PartitionSpec as P
 
+BF16 = jnp.bfloat16
+F32 = jnp.float32
+HEADS = 8
+HEAD = 64
+GROUPS = 32
+UNIT = 4
+SHAPES = ((4 * UNIT, 4 * UNIT), (3 * UNIT, 5 * UNIT), (5 * UNIT, 3 * UNIT))
+SIZES = tuple(height * breadth for height, breadth in SHAPES)
+STARTS = (0, SIZES[0], SIZES[0] + SIZES[1])
+PIX = sum(SIZES)
+EDGE = 32
+BASES = tuple(EDGE + start + i * EDGE for i, start in enumerate(STARTS))
+PADDED = PIX + 4 * EDGE
+BLOCK = 1152
+TEXT_PAD = 128
+TEXT_ROWS = 80
+SUB = 16
+NT = (((1,), (1,)), ((), ()))
+TN = (((0,), (0,)), ((), ()))
+V_IN_GAIN, V_IN_SHIFT, V_FIRST, V_EMB, V_MID_GAIN, V_MID_SHIFT, V_SECOND, V_SKIP, V_ATTN_GAIN, V_ATTN_SHIFT, V_OUT = range(11)
+
+
+def dot(left, right, dims=((1,), (0,))):
+    return lax.dot_general(left, right, (dims, ((), ())), preferred_element_type=F32)
+
+
+def group_mean(sums, count):
+    channels = sums.shape[1]
+    width = channels // GROUPS
+    lane = lax.broadcasted_iota(jnp.int32, sums.shape, 1)
+    step = 1
+    while step < width:
+        odd = lax.rem(lane // step, 2) == 1
+        sums = sums + jnp.where(odd, pltpu.roll(sums, step, 1), pltpu.roll(sums, channels - step, 1))
+        step *= 2
+    return sums / (count * width)
+
+
+def rows_of(image, i):
+    return pl.ds(pl.multiple_of(STARTS[image] + i * SUB, SUB), SUB)
+
+
+def over_rows(image, work, start):
+    return lax.fori_loop(0, SIZES[image] // SUB, lambda i, carry: work(i, rows_of(image, i), carry), start)
+
+
+def column_sum(image, channels, value):
+    def add(i, rows, carry):
+        v = value(rows)
+        return carry + (v[:8] + v[8:])
+    total = over_rows(image, add, jnp.zeros((8, channels), F32))
+    return jnp.broadcast_to(jnp.sum(total, axis=0, keepdims=True), (8, channels))
+
+
+def norm_figures(image, channels, value):
+    count = SIZES[image]
+    center = group_mean(column_sum(image, channels, value), count)[:1]
+    spread = group_mean(column_sum(image, channels, lambda rows: jnp.square(value(rows) - center)), count)[:1]
+    return center, lax.rsqrt(spread + 1e-05)
+
+
+def store_padded(pad, image, i, act):
+    breadth = SHAPES[image][1]
+    at = pl.ds(pl.multiple_of(BASES[image] + i * SUB, SUB), SUB)
+    column = lax.rem(i * SUB + lax.broadcasted_iota(jnp.int32, (SUB, 1), 0), breadth)
+    pad[0, at, :] = jnp.where(column == breadth - 1, 0.0, act).astype(BF16)
+    pad[1, at, :] = act.astype(BF16)
+    pad[2, at, :] = jnp.where(column == 0, 0.0, act).astype(BF16)
+
+
+def zero_edges(pad):
+    zeros = jnp.zeros((EDGE, pad.shape[2]), BF16)
+    for side in range(3):
+        for at in [base - EDGE for base in BASES] + [PADDED - EDGE]:
+            pad[side, at : at + EDGE, :] = zeros
+
+
+def shifted(pad, tap, image, cols, flip=False):
+    down, across = divmod(8 - tap if flip else tap, 3)
+    start = BASES[image] + (down - 1) * SHAPES[image][1] + across - 1
+    return pad[across, start : start + SIZES[image], cols]
+
+
+def gather_block(pad, q, out):
+    channels = pad.shape[2]
+    for tap in range(9):
+        low, high = max(q * BLOCK, tap * channels), min((q + 1) * BLOCK, (tap + 1) * channels)
+        if low < high:
+            for image in range(3):
+                out[STARTS[image] : STARTS[image] + SIZES[image], low - q * BLOCK : high - q * BLOCK] = shifted(
+                    pad, tap, image, slice(low - tap * channels, high - tap * channels)
+                )
+
+
+class Rows:
+    def __init__(self, parts, pix_channels, channels, text_dim, inner):
+        self.parts = parts
+        sizes = (9 * pix_channels // parts, 9 * channels // parts, pix_channels // parts, inner // parts, channels // parts, channels // parts // 2, text_dim // parts)
+        starts = [0]
+        for size in sizes:
+            starts.append(starts[-1] + size)
+        self.first, self.second, self.skip, self.out, self.attend, self.attend_more, self.text = zip(starts, sizes)
+        self.total = starts[-1]
+
+    def load(self, full, which, q, rows, buf, sem):
+        start, size = which
+        each = rows // size
+        for i in range(each):
+            pltpu.make_async_copy(full.at[q * each + i, pl.ds(start, size)], buf.at[pl.ds(i * size, size)], sem).start()
+
+    def load_attend(self, full, buf, sem):
+        start, size = self.attend
+        more, half = self.attend_more
+        def one(f, carry):
+            at = pl.multiple_of(f * size, SUB)
+            pltpu.make_async_copy(full.at[f, pl.ds(start, size)], buf.at[pl.ds(at, size), pl.ds(0, 1024)], sem).start()
+            for i in range(2):
+                pltpu.make_async_copy(
+                    full.at[f, pl.ds(more, half), pl.ds(512 * i, 512)],
+                    buf.at[pl.ds(pl.multiple_of(at + i * half, SUB), half), pl.ds(1024, 512)],
+                    sem,
+                ).start()
+            return carry
+        lax.fori_loop(0, self.parts, one, 0)
+
+
+def waited(ref, sem):
+    pltpu.make_async_copy(ref, ref, sem).wait()
+
+
+class Forward:
+    def __init__(self, rows, full, pixels, text, g_low, vec, mod, outs, scratch):
+        self.rows, self.full, self.pixels, self.text, self.g_low, self.vec, self.mod = rows, full, pixels, text, g_low, vec, mod
+        (self.o_a1, self.o_a2, self.o_mid_hat, self.o_residual, self.o_hat, self.o_normed, self.triple, self.text_pair, self.grad_attended, self.inverses) = outs
+        (self.a1, self.a2, self.patch, self.weight, self.acc0, self.acc1, self.normed, self.w_attend, self.w_skip, self.w_out, self.w_sem, self.s_sem, self.o_sem) = scratch
+
+    def out_copy(self, i, src, dst):
+        return pltpu.make_async_copy(src, dst, self.o_sem.at[i])
+
+    def row(self, r, channels=1024):
+        return self.vec[r : r + 1, :channels]
+
+    def zero(self):
+        zero_edges(self.a1)
+        zero_edges(self.a2)
+
+    def first_norm(self, image):
+        pixels, channels = self.pixels, self.pixels.shape[1]
+        value = lambda rows: pixels[rows, :].astype(F32)
+        center, inverse = norm_figures(image, channels, value)
+        gain, shift = self.row(V_IN_GAIN, channels) * inverse, self.row(V_IN_SHIFT, channels)
+        self.inverses[image : image + 1, :channels] = inverse
+        self.inverses[16 + image : 17 + image, :channels] = center
+        def act(i, rows, carry):
+            store_padded(self.a1, image, i, jax.nn.silu((value(rows) - center) * gain + shift))
+            return carry
+        over_rows(image, act, 0)
+        if image == 2:
+            self.out_copy(0, self.a1, self.o_a1).start()
+
+    def load_first(self, q):
+        self.rows.load(self.full, self.rows.first, q, BLOCK, self.weight.at[lax.rem(q, 2)], self.w_sem.at[lax.rem(q, 2)])
+
+    def load_second(self, q):
+        self.rows.load(self.full, self.rows.second, q, BLOCK, self.weight.at[lax.rem(q, 2)], self.w_sem.at[lax.rem(q, 2)])
+
+    def load_text(self, q):
+        self.rows.load(self.full, self.rows.text, q, 1024, self.weight.at[lax.rem(q, 2)], self.w_sem.at[lax.rem(q, 2)])
+
+    def conv_step(self, q, pad, acc, load, count, start):
+        @pl.when(q + 1 < count)
+        def _():
+            load(q + 1)
+        for known in range(count):
+            @pl.when(q == known)
+            def _():
+                gather_block(pad, known, self.patch)
+        par = lax.rem(q, 2)
+        waited(self.weight.at[par], self.w_sem.at[par])
+        @pl.when(q == 0)
+        def _():
+            start()
+        for col in (0, 512):
+            cols = slice(col, col + 512)
+            acc[:, cols] = acc[:, cols] + dot(self.patch[...], self.weight[par, :, cols])
+
+    def first_conv(self, q):
+        def start():
+            self.acc0[...] = jnp.zeros_like(self.acc0)
+        self.conv_step(q, self.a1, self.acc0, self.load_first, 9 * self.pixels.shape[1] // BLOCK, start)
+
+    def mid_norm(self, image):
+        acc, channels = self.acc0, self.acc0.shape[1]
+        bias = self.row(V_FIRST)
+        def shift_up(i, rows, carry):
+            acc[rows, :] = acc[rows, :] + bias
+            return carry
+        over_rows(image, shift_up, 0)
+        center, inverse = norm_figures(image, channels, lambda rows: acc[rows, :])
+        self.inverses[3 + image : 4 + image, :] = inverse
+        scale, shift = 1.0 + self.mod[image : image + 1, :channels], self.mod[image : image + 1, channels:]
+        gain, lift = self.row(V_MID_GAIN) * scale, self.row(V_MID_SHIFT) * scale + shift
+        def act(i, rows, carry):
+            hat = (acc[rows, :] - center) * inverse
+            acc[rows, :] = hat
+            store_padded(self.a2, image, i, jax.nn.silu(hat * gain + lift))
+            return carry
+        over_rows(image, act, 0)
+        if image == 2:
+            self.out_copy(1, self.a2, self.o_a2).start()
+            self.out_copy(2, self.acc0, self.o_mid_hat).start()
+
+    def load_small(self):
+        rows = self.rows
+        def one(f, carry):
+            for i, ((start, size), buf) in enumerate(((rows.skip, self.w_skip), (rows.out, self.w_out))):
+                pltpu.make_async_copy(self.full.at[f, pl.ds(start, size)], buf.at[pl.ds(pl.multiple_of(f * size, SUB), size)], self.s_sem.at[i]).start()
+            return carry
+        lax.fori_loop(0, rows.parts, one, 0)
+        rows.load_attend(self.full, self.w_attend, self.s_sem.at[2])
+
+    def skip_product(self):
+        for i, buf in enumerate((self.w_skip, self.w_out, self.w_attend)):
+            waited(buf, self.s_sem.at[i])
+        self.acc1[...] = self.acc1[...] + dot(self.pixels[...], self.w_skip[...])
+
+    def attended_grad(self):
+        self.grad_attended[...] = lax.dot_general(self.g_low[...], self.w_out[...], NT, preferred_element_type=F32).astype(BF16)
+
+    def second_conv(self, q):
+        def start():
+            self.acc1[...] = jnp.zeros_like(self.acc1)
+        self.conv_step(q, self.a2, self.acc1, self.load_second, 9 * self.acc1.shape[1] // BLOCK, start)
+
+    def last_norm(self, image):
+        acc, hats, channels = self.acc1, self.acc0, self.acc1.shape[1]
+        if image == 0:
+            self.out_copy(2, self.acc0, self.o_mid_hat).wait()
+        bias = self.row(V_SECOND) + self.row(V_SKIP)
+        def shift_up(i, rows, carry):
+            acc[rows, :] = acc[rows, :] + bias
+            return carry
+        over_rows(image, shift_up, 0)
+        center, inverse = norm_figures(image, channels, lambda rows: acc[rows, :])
+        self.inverses[6 + image : 7 + image, :] = inverse
+        gain, shift = self.row(V_ATTN_GAIN), self.row(V_ATTN_SHIFT)
+        def act(i, rows, carry):
+            hat = (acc[rows, :] - center) * inverse
+            hats[rows, :] = hat
+            self.normed[rows, :] = (hat * gain + shift).astype(BF16)
+            return carry
+        over_rows(image, act, 0)
+        if image == 2:
+            self.out_copy(3, self.acc1, self.o_residual).start()
+            self.out_copy(4, self.acc0, self.o_hat).start()
+            self.out_copy(5, self.normed, self.o_normed).start()
+
+    def project(self, i):
+        cols = slice(512 * i, 512 * (i + 1))
+        self.triple[:, cols] = dot(self.normed[...], self.w_attend[:, cols]).astype(BF16)
+
+    def text_step(self, q, total):
+        if q + 1 < 4:
+            self.load_text(q + 1)
+        par = q % 2
+        waited(self.weight.at[par, pl.ds(0, 1024)], self.w_sem.at[par])
+        part = dot(self.text[:, 1024 * q : 1024 * (q + 1)], self.weight[par, :1024, :])
+        if q:
+            part = total[...] + part
+        if q < 3:
+            total[...] = part
+        else:
+            self.text_pair[...] = jnp.zeros_like(self.text_pair)
+            for image in range(3):
+                self.text_pair[image, :TEXT_ROWS, :] = part[TEXT_ROWS * image : TEXT_ROWS * (image + 1)].astype(BF16)
+
+    def finish(self):
+        self.out_copy(0, self.a1, self.o_a1).wait()
+        self.out_copy(1, self.a2, self.o_a2).wait()
+        self.out_copy(3, self.acc1, self.o_residual).wait()
+        self.out_copy(4, self.acc0, self.o_hat).wait()
+        self.out_copy(5, self.normed, self.o_normed).wait()
+
+
 MESH = pl.DeviceIdType.MESH
-BF16=jnp.bfloat16
 DEPTH = 4
 
 
@@ -44,7 +327,13 @@
         pl.semaphore_wait(sem, self.parts)
 
 
-def gather_kernel(replicas, parts, rows, lead, own, note, emb, full, mod, notes, part, sums, n_send, n_recv, m_send, m_recv, z_send, z_recv, y_send, y_recv, s_send, s_recv, x_send, x_recv, c_send, c_recv, own_sem):
+def forward_kernel(replicas, parts, rows, lead, inner, images, *refs):
+    own, note, emb, pixels, text, g_low = refs[:6]
+    full, mod, vec, notes = refs[6:10]
+    outs = refs[10:20]
+    part, sums, text_total = refs[20:23]
+    scratch = refs[23:36]
+    (n_send, n_recv, m_send, m_recv, z_send, z_recv, y_send, y_recv, s_send, s_recv, x_send, x_recv, c_send, c_recv, own_sem) = refs[36:]
     me = Where(replicas, parts)
     span = me.span
     total, width = own.shape
@@ -143,6 +432,50 @@
             def _():
                 thin_copy(k, z).wait_recv()
                 core_copy(k, z, me.y, thin_cols).start()
+
+    def lane(k, wait):
+        half = full.at[pl.ds(0, parts // 2), at(k)]
+        whole = copy(half, half, c_send.at[k], c_recv.at[k], me.device(core=1 - me.core))
+        whole.wait_recv() if wait else whole.wait_send()
+
+    lane_in = functools.partial(lane, wait=True)
+
+    table = Rows(parts, pixels.shape[1], width, text.shape[1], inner)
+    forward = Forward(table, full, pixels, text, g_low, vec, mod, outs, scratch)
+    ready = DEPTH + 1
+    have = lambda which: (sum(which) - 1) // rows + ready
+    t1 = max(have(table.first), 5)
+    t2 = max(have(table.second), t1 + 4)
+    t3 = max(have(table.attend_more), t2 + 2)
+    t4 = max(t2 + 4, t3 + 1)
+    t5 = max(have(table.text), t4 + 1)
+    slots = max(chunks + ready, t5 + 1)
+
+    def steps(t):
+        def once(when, *work):
+            @pl.when(t == when)
+            def _():
+                for one in work:
+                    one()
+        def many(when, until, each, work):
+            @pl.when(jnp.logical_and(t >= when, t < until))
+            def _():
+                for i in range(each):
+                    work((t - when) * each + i)
+        once(0, forward.zero)
+        for image in range(3):
+            once(2 + image, functools.partial(forward.first_norm, image))
+        once(5, modulate)
+        once(t1, lambda: forward.load_first(jnp.int32(0)))
+        many(t1, t1 + 2, 2, forward.first_conv)
+        for image in range(3):
+            once(t1 + 2 + image // 2, functools.partial(forward.mid_norm, image))
+        once(t2, lambda: forward.load_second(jnp.int32(0)))
+        many(t2, t2 + 4, 2, forward.second_conv)
+        once(t3, forward.load_small)
+        once(t4, forward.skip_product, forward.attended_grad)
+        for image in range(3):
+            once(t4 + image // 2, functools.partial(forward.last_norm, image))
 
     for k in range(min(lead, chunks)):
         start_own(k)
@@ -166,6 +499,8 @@
             stage(s + 0, functools.partial(beside_thin, s=s))
         for s in range(DEPTH):
             stage(s + 1, functools.partial(beside, s=s))
+        stage(ready, lane_in)
+        steps(t)
         return carry
 
     def to_all(make):
@@ -180,10 +515,23 @@
         every.wait_send()
         every.wait_recv()
 
+    def modulate():
+        wait_all(sums, m_send, m_recv)
+        mod[...] = jnp.sum(sums[...], axis=0) + vec[V_EMB : V_EMB + 1, :]
+
     to_all(lambda far: copy(note.at[far], notes.at[me.place], n_send, n_recv, (me.group, far)))
     notes[me.place] = note[me.place]
     lax.fori_loop(0, 2, slot, 0)
     wait_all(notes, n_send, n_recv)
+    vec[...] = jnp.zeros_like(vec)
+    for row in range(V_OUT + 1):
+        size = {V_IN_GAIN: pixels.shape[1], V_IN_SHIFT: pixels.shape[1], V_EMB: emb.shape[1]}.get(row, width)
+        each = 128 * parts // size
+        for block in range(size // 128):
+            value = notes[block * each, images + row : images + row + 1, :].astype(jnp.float32)
+            for i in range(1, each):
+                value = value + notes[block * each + i, images + row : images + row + 1, :].astype(jnp.float32)
+            vec[row : row + 1, block * 128 : (block + 1) * 128] = value
     rows_in = notes.shape[1]
     step = 512
     for at_col in range(0, emb.shape[1], step):
@@ -192,10 +540,13 @@
         part[:, :, cols] = product.reshape(parts, rows_in, step)[:, :8]
     to_all(lambda far: copy(part.at[far], sums.at[me.place], m_send, m_recv, (me.group, far)))
     sums[me.place] = part[me.place]
-    lax.fori_loop(2, chunks + DEPTH, slot, 0)
     local.wait()
-    wait_all(sums, m_send, m_recv)
-    mod[...] = jnp.sum(sums[...], axis=0)
+    lax.fori_loop(2, slots, slot, 0)
+    forward.load_text(jnp.int32(0))
+    for i in range(3):
+        forward.project(i)
+    for q in range(4):
+        forward.text_step(q, text_total)
 
     def finish(k, carry):
         for step, edge in ((1, me.z < DEPTH - 1), (-1, me.z > 0)):
@@ -211,46 +562,50 @@
             @pl.when(z != me.z)
             def _():
                 thin_copy(k, z).wait_send()
-        lane = full.at[pl.ds(0, parts // 2), at(k)]
-        whole = copy(lane, lane, c_send.at[k], c_recv.at[k], me.device(core=1 - me.core))
-        whole.wait_send()
-        whole.wait_recv()
+        lane(k, False)
         return carry
 
     lax.fori_loop(0, chunks, finish, 0)
-
-
-def gather_all(own, note, emb, replicas, parts, rows=80, lead=3):
-    wide = emb.shape[1]
+    forward.finish()
+
+
+def forward_all(own, note, emb, pixels, text, g_low, images, inner, replicas, parts, rows=80, lead=3):
     total, width = own.shape
     chunks = total // rows
     span = parts // (2 * DEPTH)
+    pix, pix_width = pixels.shape
     dma = lambda *shape: pltpu.SemaphoreType.DMA(shape)
+    bf = lambda *shape: jax.ShapeDtypeStruct(shape, BF16)
+    fl = lambda *shape: jax.ShapeDtypeStruct(shape, F32)
+    hbm, vmem = pl.BlockSpec(memory_space=pl.ANY), pl.BlockSpec(memory_space=pltpu.VMEM)
     return pl.pallas_call(
-        functools.partial(gather_kernel, replicas, parts, rows, lead),
+        functools.partial(forward_kernel, replicas, parts, rows, lead, inner, images),
         out_shape=[
-            jax.ShapeDtypeStruct((parts, total, width), own.dtype),
-            jax.ShapeDtypeStruct((8, wide), jnp.float32),
-            jax.ShapeDtypeStruct(note.shape, note.dtype),
+            bf(parts, total, width), fl(8, emb.shape[1]), fl(16, emb.shape[1]), bf(*note.shape),
+            bf(3, PADDED, pix_width), bf(3, PADDED, width), fl(pix, width), fl(pix, width), fl(pix, width), bf(pix, width),
+            bf(pix, 3 * inner), bf(3, TEXT_PAD, 2 * inner), bf(pix, inner), fl(24, width),
         ],
-        in_specs=[pl.BlockSpec(memory_space=pl.ANY)] + [pl.BlockSpec(memory_space=pltpu.VMEM)] * 2,
-        out_specs=[pl.BlockSpec(memory_space=pl.ANY)] + [pl.BlockSpec(memory_space=pltpu.VMEM)] * 2,
+        in_specs=[hbm] + [vmem] * 5,
+        out_specs=[hbm, vmem, vmem, vmem] + [hbm] * 6 + [vmem] * 4,
         scratch_shapes=[
-            pltpu.VMEM((parts, 8, wide), jnp.float32),
-            pltpu.VMEM((parts, 8, wide), jnp.float32),
+            pltpu.VMEM((parts, 8, emb.shape[1]), F32),
+            pltpu.VMEM((parts, 8, emb.shape[1]), F32),
+            pltpu.VMEM((text.shape[0], width), F32),
+            pltpu.VMEM((3, PADDED, pix_width), BF16), pltpu.VMEM((3, PADDED, width), BF16),
+            pltpu.VMEM((pix, BLOCK), BF16), pltpu.VMEM((2, BLOCK, width), BF16),
+            pltpu.VMEM((pix, width), F32), pltpu.VMEM((pix, width), F32), pltpu.VMEM((pix, width), BF16),
+            pltpu.VMEM((width, 3 * inner), BF16), pltpu.VMEM((pix_width, width), BF16), pltpu.VMEM((inner, width), BF16),
+            dma(2), dma(3), dma(6),
             dma(), dma(), dma(), dma(),
             dma(chunks, DEPTH, 2), dma(chunks, DEPTH),
             dma(chunks, DEPTH, span - 1), dma(chunks, DEPTH, span - 1),
             dma(chunks, DEPTH), dma(chunks, DEPTH),
             dma(chunks, DEPTH, span - 1), dma(chunks, DEPTH, span - 1),
-            dma(chunks), dma(chunks), pltpu.SemaphoreType.DMA,
+            dma(chunks), dma(chunks), dma(),
         ],
-        compiler_params=pltpu.CompilerParams(collective_id=0, has_side_effects=True, vmem_limit_bytes=40 << 20),
-        name="gather_all",
-    )(own, note, emb)
-
-
-F32=jnp.float32
+        compiler_params=pltpu.CompilerParams(collective_id=0, has_side_effects=True, vmem_limit_bytes=60 << 20),
+        name="forward_all",
+    )(own, note, emb, pixels, text, g_low)
 
 
 class Seat(Where):
@@ -500,24 +855,11 @@
     )(*views, note)
 
 
-HEADS = 8
-HEAD = 64
-GROUPS = 32
-UNIT = 4
-SHAPES = ((4 * UNIT, 4 * UNIT), (3 * UNIT, 5 * UNIT), (5 * UNIT, 3 * UNIT))
-SIZES = tuple(height * breadth for height, breadth in SHAPES)
-STARTS = (0, SIZES[0], SIZES[0] + SIZES[1])
-
-
-def dot(left, right, dims=((1,), (0,))):
-    return lax.dot_general(left, right, (dims, ((), ())), preferred_element_type=F32)
-
-
 def images(rows):
     return [rows[start : start + size] for start, size in zip(STARTS, SIZES)]
 
 
-def group_mean(column_sums, count):
+def flat_group_mean(column_sums, count):
     channels = column_sums.shape[-1]
     width = channels // GROUPS
     totals = jnp.sum(column_sums.reshape(GROUPS, width), axis=1, keepdims=True) / (count * width)
@@ -526,8 +868,8 @@
 
 def normalise(rows):
     count = rows.shape[0]
-    centered = rows - group_mean(jnp.sum(rows, axis=0), count)
-    spread = group_mean(jnp.sum(jnp.square(centered), axis=0), count)
+    centered = rows - flat_group_mean(jnp.sum(rows, axis=0), count)
+    spread = flat_group_mean(jnp.sum(jnp.square(centered), axis=0), count)
     inverse = lax.rsqrt(spread + 1e-05)
     return centered * inverse, inverse
 
@@ -536,8 +878,8 @@
     count = grad.shape[0]
     plain = jnp.sum(grad, axis=0)
     crossed = jnp.sum(grad * hat, axis=0)
-    mean_plain = group_mean(plain * factor, count)
-    mean_crossed = group_mean(crossed * factor, count)
+    mean_plain = flat_group_mean(plain * factor, count)
+    mean_crossed = flat_group_mean(crossed * factor, count)
     return inverse * (grad * factor[None, :] - mean_plain - hat * mean_crossed), plain, crossed
 
 
@@ -560,9 +902,6 @@
             windows = windows[::-1]
         parts.append(jnp.concatenate(windows, axis=-1).reshape(height * breadth, 9 * channels))
     return jnp.concatenate(parts, 0)
-
-
-TEXT_PAD = 128
 
 
 def attention_kernel(q_ref, k_ref, v_ref, tk_ref, tv_ref, mask_ref, go_ref, o_ref, dq_ref, dk_ref, dv_ref, dtk_ref, dtv_ref):
@@ -642,6 +981,20 @@
     )(triple, triple, triple, text_pair, text_pair, mask, grad_attended)
 
 
+def fold_attend(part, width):
+    more = part[..., width:]
+    half = part.shape[-2] // 2
+    return [part[..., :width], jnp.concatenate([more[..., :half, :], more[..., half:, :]], -1)]
+
+
+def unfold_attend(part, columns):
+    blocks, rows, width = part.shape
+    size = rows * 2 // 3
+    more = part[:, size:]
+    half = columns - width
+    return jnp.concatenate([part[:, :size], jnp.concatenate([more[..., :half], more[..., half:]], 1)], -1).reshape(blocks * size, columns)
+
+
 def body(
     pixels,
     embedding,
@@ -679,65 +1032,55 @@
     emb_cut = jnp.pad(emb_cut, ((0, 0), (0, 0), (0, 128 - depth)))
 
     vectors = (in_gain, in_shift, first_bias, emb_bias, mid_gain, mid_shift, second_bias, skip_bias, attn_gain, attn_shift, out_bias)
-    flat = jnp.concatenate(vectors)
-    room = 16 - images_here
-    flat = jnp.pad(flat, (0, room * 128 - flat.shape[0])).reshape(1, room, 128)
-    note = jnp.concatenate([emb_cut, jnp.broadcast_to(flat, (parts, room, 128))], 1)
-    small = jnp.concatenate([skip_weight, out_weight, attend_weight.reshape(-1, skip_weight.shape[1])], 0)
-    own = jnp.concatenate([conv_first, conv_second, text_weight, small], 0)
-    full, modulation, notes = gather_all(own, note, jnp.pad(emb_weight, ((0, 128 - depth), (0, 0))), replicas, parts)
-    packed = notes[:, images_here:].reshape(parts, -1).astype(F32)
-    whole = []
-    at = 0
+    lane = lax.broadcasted_iota(jnp.int32, (1, 128), 1)
+    lines = []
     for vector in vectors:
-        whole.append(packed[:, at : at + vector.shape[0]].reshape(-1))
-        at += vector.shape[0]
-    (in_gain, in_shift, first_bias, emb_bias, mid_gain, mid_shift, second_bias, skip_bias, attn_gain, attn_shift, out_bias) = whole
-    modulation = modulation[:images_here] + emb_bias
-
-    cuts = []
-    at = 0
-    for part in (conv_first, conv_second, text_weight, skip_weight, out_weight):
-        size = part.shape[0]
-        cuts.append(full[:, at : at + size].reshape(parts * size, -1))
-        at += size
-    attend_width = attend_weight.shape[1]
-    attend_weight = full[:, at:].reshape(-1, attend_width)
-    conv_first, conv_second, text_weight, skip_weight, out_weight = cuts
-    channels = conv_first.shape[1]
-    inner = out_weight.shape[0]
-    scale, shift = modulation[:, :channels], modulation[:, channels:]
-
-    pixel_hat = [normalise(part.astype(F32)) for part in images(pixels)]
-    first_pre = [hat * in_gain + in_shift for hat, _ in pixel_hat]
-    first_act = jnp.concatenate([jax.nn.silu(part) for part in first_pre], 0).astype(BF16)
-    first_patches = patches(first_act)
-    first_conv = dot(first_patches, conv_first) + first_bias
-    mid_hat = [normalise(part) for part in images(first_conv)]
-    mid_pre = [
-        (hat * mid_gain + mid_shift) * (1.0 + scale[i]) + shift[i]
-        for i, (hat, _) in enumerate(mid_hat)
-    ]
-    second_act = jnp.concatenate([jax.nn.silu(part) for part in mid_pre], 0).astype(BF16)
-    second_patches = patches(second_act)
-    residual = dot(pixels, skip_weight) + dot(second_patches, conv_second) + (skip_bias + second_bias)
-    attn_hat = [normalise(part) for part in images(residual)]
-    normed = jnp.concatenate([hat * attn_gain + attn_shift for hat, _ in attn_hat], 0).astype(BF16)
-    triple = dot(normed, attend_weight).astype(BF16)
-    text_len = text_states.shape[1]
-    text_rows = text_states.reshape(3 * text_len, -1)
-    text_pair = dot(text_rows, text_weight).astype(BF16).reshape(3, text_len, -1)
-    text_pair = jnp.pad(text_pair, ((0, 0), (0, TEXT_PAD - text_len), (0, 0)))
-    mask = jnp.pad(
-        (text_mask > 0).astype(jnp.int32), ((0, 0), (0, TEXT_PAD - text_len)), constant_values=2
-    )
+        size = vector.shape[0]
+        wide = jnp.tile(vector, 128 // size).reshape(1, 128)
+        lines.append(jnp.where(lane // size == lax.rem(place, 128 // size), wide, jnp.zeros_like(wide)))
+    room = 16 - images_here - len(lines)
+    flat = jnp.concatenate(lines + [jnp.zeros((room, 128), BF16)] if room else lines, 0)[None]
+    note = jnp.concatenate([emb_cut, jnp.broadcast_to(flat, (parts,) + flat.shape[1:])], 1)
+    channels = skip_weight.shape[1]
+    inner = out_weight.shape[0] * parts
+    own = jnp.concatenate([conv_first, conv_second, skip_weight, out_weight] + fold_attend(attend_weight, channels) + [text_weight], 0)
     present = jnp.concatenate(
         [jnp.broadcast_to(occupancy[0, i].astype(F32), (SIZES[i], 1)) for i in range(3)], 0
     )
     grad_out = cotangent.astype(F32) * present
     grad_low = grad_out.astype(BF16)
-    grad_attended = dot(grad_low, out_weight, ((1,), (1,))).astype(BF16)
+    text_len = text_states.shape[1]
+    text_rows = jnp.pad(text_states, ((0, 0), (0, TEXT_ROWS - text_len), (0, 0))).reshape(3 * TEXT_ROWS, -1)
+    (full, modulation, vec, _, act1, act2, mid_hats, residual, hats, normed, triple, text_pair, grad_attended, inverses) = forward_all(
+        own, note, jnp.pad(emb_weight, ((0, 128 - depth), (0, 0))), pixels, text_rows, grad_low, images_here, inner, replicas, parts)
+    scale, shift = modulation[:images_here, :channels], modulation[:images_here, channels:]
+    in_gain, in_shift = vec[V_IN_GAIN, : pixels.shape[1]], vec[V_IN_SHIFT, : pixels.shape[1]]
+    mid_gain, mid_shift, attn_gain, out_bias = (vec[row, :channels] for row in (V_MID_GAIN, V_MID_SHIFT, V_ATTN_GAIN, V_OUT))
+    table = Rows(parts, pixels.shape[1], channels, text_states.shape[2], inner)
+    cut = lambda which: full[:, which[0] : sum(which)].reshape(parts * which[1], -1)
+    conv_first, conv_second, skip_weight, out_weight = (cut(which) for which in (table.first, table.second, table.skip, table.out))
+    attend_weight = unfold_attend(full[:, table.attend[0] : sum(table.attend_more)], 3 * inner)
+
+    middles = lambda act: jnp.concatenate([act[1, base : base + size] for base, size in zip(BASES, SIZES)], 0)
+    first_act, second_act = middles(act1), middles(act2)
+    pixel_hat = [
+        ((part.astype(F32) - inverses[16 + i, : pixels.shape[1]]) * inverses[i, : pixels.shape[1]], inverses[i, : pixels.shape[1]])
+        for i, part in enumerate(images(pixels))
+    ]
+    first_pre = [hat * in_gain + in_shift for hat, _ in pixel_hat]
+    first_patches = patches(first_act)
+    mid_hat = [(part, inverses[3 + i]) for i, part in enumerate(images(mid_hats))]
+    mid_pre = [
+        (hat * mid_gain + mid_shift) * (1.0 + scale[i]) + shift[i]
+        for i, (hat, _) in enumerate(mid_hat)
+    ]
+    second_patches = patches(second_act)
+    attn_hat = [(part, inverses[6 + i]) for i, part in enumerate(images(hats))]
+    mask = jnp.pad(
+        (text_mask > 0).astype(jnp.int32), ((0, 0), (0, TEXT_PAD - text_len)), constant_values=2
+    )
     attended, dq, dk, dv, dtk, dtv = attention(triple, text_pair, mask, grad_attended)
+    text_rows = text_states.reshape(3 * text_len, -1)
     block_output = (present * (residual + (dot(attended, out_weight) + out_bias))).astype(BF16)
 
     tn = ((0,), (0,))
@@ -807,21 +1150,21 @@
     note = jnp.concatenate(
         [jnp.broadcast_to(mod_rows, (parts,) + mod_rows.shape[1:]).astype(BF16), emb_cut, cut.astype(BF16)], 1
     )
-    pack = lambda part: part.reshape(parts, -1, channels)
+    pack = lambda part: part.astype(BF16).reshape(parts, -1, part.shape[-1])
     grad_small = jnp.concatenate(
-        [pack(grad_skip_weight), pack(grad_out_weight), pack(grad_attend_weight)], 1
-    ).astype(BF16).reshape(-1, channels)
+        [pack(grad_skip_weight), pack(grad_out_weight)] + fold_attend(pack(grad_attend_weight), channels), 1
+    ).reshape(-1, channels)
     owned, notes = reduce_all(
         [grad_conv_first.astype(BF16), grad_conv_second.astype(BF16), grad_text_weight.astype(BF16), grad_small],
         note, replicas, parts, 512 // parts,
     )
     at = 0
     cuts = []
-    for size in (conv_first.shape[0], conv_second.shape[0], text_weight.shape[0], skip_weight.shape[0], out_weight.shape[0]):
+    for size in (conv_first.shape[0], conv_second.shape[0], text_weight.shape[0] * parts, skip_weight.shape[0], out_weight.shape[0]):
         cuts.append(owned[at : at + size // parts])
         at += size // parts
     grad_conv_first, grad_conv_second, grad_text_weight, grad_skip_weight, grad_out_weight = cuts
-    grad_attend_weight = owned[at:].reshape(-1, attend_width)
+    grad_attend_weight = unfold_attend(owned[None, at:], 3 * inner)
     mod_rows = notes[:, :mod_count].reshape(-1, 2 * channels)
     all_act = notes[:, mod_count : mod_count + images_here, :depth].reshape(-1, depth)
     grad_emb_weight = dot(all_act, mod_rows, tn)

time: 1060 us -> 1070 us (level)
  Pallas kernels: 426 us -> 487 us
  matrix products: 141 us -> 87.1 us
  local copies, waits for them, and re-layouts: 396 us -> 414 us
  other arithmetic: 76.2 us -> 59.8 us
    pallas_call x1, Pallas kernels: 197 us -> 259 us  [forward_all(): pl.pallas_call(functools.partial(forward_kernel, replicas, parts, rows, l...]
    dot_general x16 -> x10, matrix products: 107 us -> 54.4 us  [dot(): lax.dot_general(left, right, (dims, ((), ())), preferred_element_type=F32)]
    unnamed x371 -> x315, local copies, waits for them, and re-layouts: 84.6 us -> 130 us
    reshape x27 -> x0, local copies, waits for them, and re-layouts: 14.4 us -> none  [the longest x1 6.21 us: body(): attend_weight = full[:, at:].reshape(-1, attend_width)]
    concatenate x3 -> x2, local copies, waits for them, and re-layouts: 13.7 us -> 0.9 us  [the longest x1 0.84 us: body(): jnp.concatenate([conv_first, conv_second, skip_weight, out_weight] + fold...]
    reduce_sum x33 -> x5, other arithmetic: 13.8 us -> 1.25 us  [flat_group_mean(): jnp.sum(column_sums.reshape(GROUPS, width), axis=1, keepdims=True)]
    concatenate x76, local copies, waits for them, and re-layouts: 119 us -> 107 us  [patches(): jnp.concatenate(windows, axis=-1).reshape(height * breadth, 9 * channels)]
    slice x12, local copies, waits for them, and re-layouts: 32.2 us -> 43.7 us  [patches(): padded[down:down + height, across:across + breadth]]
where the time goes in v2:
time: 1070 us; the launch traced here: 1050 us
  Pallas kernels  487 us (46%)
  local copies, waits for them, and re-layouts  414 us (39%)
  matrix products  87.1 us (8%)
  other arithmetic  59.8 us (6%)
    pallas_call x1, Pallas kernels, forward_all(): pl.pallas_call(functools.partial(forward_kernel, replicas, parts, rows, l...  259 us
    pallas_call x1, Pallas kernels, reduce_all(): pl.pallas_call(functools.partial(reduce_kernel, replicas, parts, rows, sp...  204 us
    unnamed x315, local copies, waits for them, and re-layouts  130 us
    concatenate x76, local copies, waits for them, and re-layouts, patches(): jnp.concatenate(windows, axis=-1).reshape(height * breadth, 9 * channels)  107 us
    dot_general x10, matrix products, dot(): lax.dot_general(left, right, (dims, ((), ())), preferred_element_type=F32)  54.4 us
    slice x12, local copies, waits for them, and re-layouts, patches(): padded[down:down + height, across:across + breadth]  43.7 us
    concatenate x2, local copies, waits for them, and re-layouts, patches(): return jnp.concatenate(parts, 0)  36.7 us
    slice x3, local copies, waits for them, and re-layouts, body(): full[:, which[0]:sum(which)].reshape(parts * which[1], -1)  30.2 us

profile of v2, /device:TPU:0, one launch (start us, length us, event | category | flops | bytes accessed | tf_op | source)
XLA Modules:
  0.0 1052.7 jit_solution(3477517229532108792)
XLA Ops:
  0.8 2.1 constant_dynamic-update-slice_fusion.6
  2.9 2.5 constant_dynamic-update-slice_fusion.5
  14.0 3.1 pad.55
  21.2 259.3 %forward_all.1 = (bf16[16,1280,1024]{2,1,0:T(8,128)(2,1)}, f32[8,2048]{1,0:T(8,128)}, f32[16,2048]{1,0:T(8,128)}, bf16[16,16,128]{2,1,0:T(8,128)(2,1)}, bf16[3,8...) custom-call(bf16[1280,1024]{1,0:T(8,128)(2,1)} %constant_dynamic-upd, ...), custom_call_target="tpu_custom_call" | custom-call | tf_op jit(solution)/shard_map/forward_all/pallas_call | solution.py:581
  284.5 24.2 %shard_map.383 = (bf16[736,512]{1,0:T(8,128)(2,1)S(1)}, bf16[736,512]{1,0:T(8,128)(2,1)S(1)}, bf16[736,512]{1,0:T(8,128)(2,1)S(1)}, bf16[736,512]{1,0:T(8,128)(2...) custom-call(bf16[736,1536]{1,0:T(8,128)(2,1)S(1)} %copy-done, bf16[736,1536]{1,0:T(8,128)(2,1)S(1)} %copy-done, ...), custom_call_target="tpu_custom_call" | custom-call | tf_op jit(solution)/shard_map/pallas_call | solution.py:966
  309.5 3.4 fusion.45
  313.4 2.8 fusion.37
  316.2 4.3 multiply_convert_fusion
  324.1 2.1 fusion.46
  328.5 2.5 fusion.59
  339.2 3.2 subtract_multiply_fusion.5
  344.2 3.2 fusion.11
  349.1 5.9 pad_slice_fusion.48
  368.3 5.2 pad_slice_fusion.72
  373.5 2.0 concatenate.368
  418.4 5.5 pad_maximum_fusion
  423.8 18.4 %copy.47 = bf16[736,9216]{0,1:T(8,128)(2,1)} copy(bf16[736,9216]{1,0:T(8,128)(2,1)} %pad_maximum_fusion) | data formatting | bytes 27131904 | tf_op jit(solution)/shard_map/concatenate | solution.py:904
  442.2 17.9 %slice.655 = bf16[16,576,1024]{2,1,0:T(8,128)(2,1)} slice(bf16[16,1280,1024]{2,1,0:T(8,128)(2,1)} %get-tuple-element.46), slice={[0:16], [288:864], [0:1024]} | slice | bytes 37748736 | tf_op jit(solution)/shard_map/slice | solution.py:1060
  460.1 19.1 %convolution_bitcast_fusion = f32[736,1024]{1,0:T(8,128)} fusion(bf16[736,9,1024]{0,2,1:T(8,128)(2,1)S(1)} %bitcast.141, bf16[9,1024,1024]{2,1,0:T(8,128)(2,1)} %bitcast.139), kind=kOutput, calls=%fused_computation.24 | convolution fusion | flops 13891534848 | bytes 35454976 | tf_op jit(solution)/shard_map/dot_general | solution.py:1107
  480.7 4.4 multiply_reduce_fusion.3
  487.0 3.2 fusion.23
  491.3 5.6 pad_slice_fusion.64
  521.2 5.8 pad_slice_fusion.40
  535.9 2.0 concatenate.391
  547.4 3.1 fusion.40
  551.1 2.6 fusion.21
  555.5 5.6 pad_maximum_fusion.1
  561.1 18.4 %copy.49 = bf16[736,9216]{0,1:T(8,128)(2,1)} copy(bf16[736,9216]{1,0:T(8,128)(2,1)} %pad_maximum_fusion.1) | data formatting | bytes 27131904 | tf_op jit(solution)/shard_map/concatenate | solution.py:904
  579.5 8.9 slice.699
  588.4 13.5 %convolution_bitcast_fusion.1 = f32[736,512]{1,0:T(8,128)S(1)} fusion(bf16[736,9,1024]{0,2,1:T(8,128)(2,1)} %bitcast.140, bf16[9,512,1024]{2,1,0:T(8,128)(2,1)} %bitcast.143), kind=kOutput, calls=%fused_computation.33 | convolution fusion | flops 6945767424 | bytes 24510464 | tf_op jit(solution)/shard_map/dot_general | solution.py:1130
  606.5 2.4 subtract_multiply_fusion.10
  610.5 3.6 maximum_add_fusion.1
  616.6 3.7 pad_slice_fusion.80
  634.7 3.9 pad_slice_fusion.88
  676.7 9.8 convolution_convert_fusion.1
  686.6 2.0 fusion.47
  689.5 6.1 pad_slice_fusion.32
  711.8 5.6 pad_slice_fusion.56
  732.8 2.2 bitcast_dynamic-update-slice_fusion.2
  774.1 20.5 %convolution_convert_fusion = bf16[9216,1024]{1,0:T(8,128)(2,1)} fusion(bf16[736,1024]{1,0:T(8,128)(2,1)S(1)} %get-tuple-element.129, bf16[240,9216]{1,0:T(8,128)(2,1)} %constant_dynamic-update-slice_fusion.104, bf16[240,9216]{1,0:T(8,128)(2,1)} %constant_dynamic-update-slice_fusion.96, bf16[256,9216]{1,0:T(8,128)(2,1)} %constant_dynamic-update-slice_fusion.88), kind=kOutput, calls=%fused_computation | convolution fusion | flops 13941669888 | bytes 33947648 | tf_op jit(solution)/shard_map/dot_general | solution.py:33
  794.6 5.6 fusion.10
  800.2 12.2 %copy.51 = bf16[4096,1024]{1,0:T(8,128)(2,1)} copy(bf16[4096,1024]{0,1:T(8,128)(2,1)} %fusion.10) | data formatting | bytes 16777216 | tf_op jit(solution)/shard_map/convert_element_type | solution.py:1158
  812.4 4.8 convolution_convert_fusion.2
  821.1 6.4 pad_maximum_fusion.2.refs_3_
  830.0 203.9 %reduce_all.1 = (f32[1280,1024]{1,0:T(8,128)}, bf16[32,64,128]{2,1,0:T(8,128)(2,1)}) custom-call(bf16[4,2,2,288,1024]{4,3,2,1,0:T(8,128)(2,1)} %bitcast.142, bf16[4,2,2,576,1024]{4,3,2,1,0:T(8,128)(2,1)} %bitcast.138, bf16[4,2,2,256,1024]{4,3,2,1,0:T(8,128)(2,1)} %bitcast.137, bf16[4,2,2,160,1024]{4,3,2,1,0:T(8,128)(2,1)} %pad_maximum_fusion.2.refs_3_, ...), custom_call_target="tpu_custom_call" | custom-call | tf_op jit(solution)/shard_map/reduce_all/pallas_call | solution.py:830
  1035.5 2.4 slice.775
  1042.5 3.4 slice.781
  1049.4 2.3 slice.790
  (604 shorter events, 287.5 us)
Async XLA Ops:
  0.7 10.6 %copy-start.22 = (bf16[256,1024]{1,0:T(8,128)(2,1)S(1)}, bf16[256,1024]{1,0:T(8,128)(2,1)}, u32[]{:S(2)}) copy-start(bf16[256,1024]{1,0:T(8,128)(2,1)} %param.45) | copy-start | bytes 1572868
  0.7 11.4 %copy-start.88 = (bf16[32]{0:T(256)(128)(2,1)S(1)}, bf16[32]{0:T(256)(128)(2,1)}, u32[]{:S(2)}) copy-start(bf16[32]{0:T(256)(128)(2,1)} %param.31) | copy-start | bytes 196
  0.7 11.5 %copy-start.89 = (bf16[32]{0:T(256)(128)(2,1)S(1)}, bf16[32]{0:T(256)(128)(2,1)}, u32[]{:S(2)}) copy-start(bf16[32]{0:T(256)(128)(2,1)} %param.30) | copy-start | bytes 196
  0.7 11.6 %copy-start.90 = (bf16[64]{0:T(256)(128)(2,1)S(1)}, bf16[64]{0:T(256)(128)(2,1)}, u32[]{:S(2)}) copy-start(bf16[64]{0:T(256)(128)(2,1)} %param.36) | copy-start | bytes 388
  0.7 11.7 %copy-start.91 = (bf16[64]{0:T(256)(128)(2,1)S(1)}, bf16[64]{0:T(256)(128)(2,1)}, u32[]{:S(2)}) copy-start(bf16[64]{0:T(256)(128)(2,1)} %param.33) | copy-start | bytes 388
  0.7 11.8 %copy-start.92 = (bf16[128]{0:T(256)(128)(2,1)S(1)}, bf16[128]{0:T(256)(128)(2,1)}, u32[]{:S(2)}) copy-start(bf16[128]{0:T(256)(128)(2,1)} %param.35) | copy-start | bytes 772
  0.7 11.8 %copy-start.93 = (bf16[64]{0:T(256)(128)(2,1)S(1)}, bf16[64]{0:T(256)(128)(2,1)}, u32[]{:S(2)}) copy-start(bf16[64]{0:T(256)(128)(2,1)} %param.39) | copy-start | bytes 388
  0.7 11.9 %copy-start.94 = (bf16[64]{0:T(256)(128)(2,1)S(1)}, bf16[64]{0:T(256)(128)(2,1)}, u32[]{:S(2)}) copy-start(bf16[64]{0:T(256)(128)(2,1)} %param.37) | copy-start | bytes 388
  0.7 12.0 %copy-start.95 = (bf16[64]{0:T(256)(128)(2,1)S(1)}, bf16[64]{0:T(256)(128)(2,1)}, u32[]{:S(2)}) copy-start(bf16[64]{0:T(256)(128)(2,1)} %param.42) | copy-start | bytes 388
  0.8 12.1 %copy-start.96 = (bf16[64]{0:T(256)(128)(2,1)S(1)}, bf16[64]{0:T(256)(128)(2,1)}, u32[]{:S(2)}) copy-start(bf16[64]{0:T(256)(128)(2,1)} %param.41) | copy-start | bytes 388
  0.8 12.2 %copy-start.97 = (bf16[64]{0:T(256)(128)(2,1)S(1)}, bf16[64]{0:T(256)(128)(2,1)}, u32[]{:S(2)}) copy-start(bf16[64]{0:T(256)(128)(2,1)} %param.47) | copy-start | bytes 388
  0.8 12.3 %copy-start.98 = (bf16[64]{0:T(256)(128)(2,1)S(1)}, bf16[64]{0:T(256)(128)(2,1)}, u32[]{:S(2)}) copy-start(bf16[64]{0:T(256)(128)(2,1)} %param.43) | copy-start | bytes 388
  0.8 12.5 %copy-start.71 = (bf16[3,2048]{1,0:T(4,128)(2,1)S(1)}, bf16[3,2048]{1,0:T(4,128)(2,1)}, u32[]{:S(2)}) copy-start(bf16[3,2048]{1,0:T(4,128)(2,1)} %param.25) | copy-start | bytes 36868
  2.9 14.2 %copy-start.84 = (s32[1,3]{1,0:T(1,128)S(1)}, s32[1,3]{1,0:T(1,128)}, u32[]{:S(2)}) copy-start(s32[1,3]{1,0:T(1,128)} %param.28) | copy-start | bytes 40
  2.9 16.9 %copy-start.12 = (bf16[736,1024]{1,0:T(8,128)(2,1)S(1)}, bf16[736,1024]{1,0:T(8,128)(2,1)}, u32[]{:S(2)}) copy-start(bf16[736,1024]{1,0:T(8,128)(2,1)} %param.29) | copy-start | bytes 4521988
  13.3 267.2 %copy-start.24 = (bf16[16,3,128]{2,1,0:T(4,128)(2,1)}, bf16[16,3,128]{2,1,0:T(4,128)(2,1)S(1)}, u32[]{:S(2)}) copy-start(bf16[16,3,128]{2,1,0:T(4,128)(2,1)S(1)} %fusion.30) | copy-start | bytes 36868
  21.2 259.3 %copy-start.85 = (s32[3,77]{1,0:T(4,128)S(1)}, s32[3,77]{1,0:T(4,128)}, u32[]{:S(2)}) copy-start(s32[3,77]{1,0:T(4,128)} %param.27) | copy-start | bytes 2776
  309.4 11.0 %copy-start.3 = (bf16[736,512]{1,0:T(8,128)(2,1)}, bf16[736,512]{1,0:T(8,128)(2,1)S(1)}, u32[]{:S(2)}) copy-start(bf16[736,512]{1,0:T(8,128)(2,1)S(1)} %get-tuple-element.45) | copy-start | bytes 2260996
  332.9 9.5 copy-start.35
  332.9 9.5 copy-start.37
  398.6 15.2 %copy-start.17 = (bf16[12,20,1024]{2,1,0:T(8,128)(2,1)S(1)}, bf16[12,20,1024]{2,1,0:T(8,128)(2,1)}, u32[]{:S(2)}) copy-start(bf16[12,20,1024]{2,1,0:T(8,128)(2,1)} %get-tuple-element.186) | copy-start | bytes 1474564
  401.4 9.6 copy-start.19
  442.2 17.9 %copy-start.7 = (bf16[736,9216]{0,1:T(8,128)(2,1)S(1)}, bf16[736,9216]{0,1:T(8,128)(2,1)}, u32[]{:S(2)}) copy-start(bf16[736,9216]{0,1:T(8,128)(2,1)} %copy.47) | copy-start | bytes 40697860
  460.1 20.6 %copy-start.78 = (f32[1,1024]{1,0:T(1,128)S(1)}, f32[1,1024]{1,0:T(1,128)}, u32[]{:S(2)}) copy-start(f32[1,1024]{1,0:T(1,128)} %get-tuple-element.281) | copy-start | bytes 12292
  460.1 20.6 %copy-start.79 = (f32[1,1024]{1,0:T(1,128)S(1)}, f32[1,1024]{1,0:T(1,128)}, u32[]{:S(2)}) copy-start(f32[1,1024]{1,0:T(1,128)} %get-tuple-element.282) | copy-start | bytes 12292
  460.1 20.6 %copy-start.80 = (f32[1,1024]{1,0:T(1,128)S(1)}, f32[1,1024]{1,0:T(1,128)}, u32[]{:S(2)}) copy-start(f32[1,1024]{1,0:T(1,128)} %get-tuple-element.283) | copy-start | bytes 12292
  490.2 22.1 %copy-start.13 = (bf16[240,1024]{1,0:T(8,128)(2,1)}, bf16[240,1024]{1,0:T(8,128)(2,1)S(1)}, u32[]{:S(2)}) copy-start(bf16[240,1024]{1,0:T(8,128)(2,1)S(1)} %get-tuple-element.132) | copy-start | bytes 1474564
  490.2 44.9 %copy-start.15 = (bf16[240,1024]{1,0:T(8,128)(2,1)}, bf16[240,1024]{1,0:T(8,128)(2,1)S(1)}, u32[]{:S(2)}) copy-start(bf16[240,1024]{1,0:T(8,128)(2,1)S(1)} %get-tuple-element.133) | copy-start | bytes 1474564
  535.1 12.3 %copy-start.67 = (f32[1,1024]{1,0:T(1,128)S(1)}, f32[1,1024]{1,0:T(1,128)}, u32[]{:S(2)}) copy-start(f32[1,1024]{1,0:T(1,128)} %get-tuple-element.286) | copy-start | bytes 12292
  541.8 8.7 copy-start.75
  541.8 9.3 copy-start.68
  588.3 13.6 %copy-start.10 = (bf16[736,512]{1,0:T(8,128)(2,1)S(1)}, bf16[736,512]{1,0:T(8,128)(2,1)}, u32[]{:S(2)}) copy-start(bf16[736,512]{1,0:T(8,128)(2,1)} %refs_3_.1) | copy-start | bytes 2260996
  588.3 13.6 %copy-start.34 = (f32[1,512]{1,0:T(1,128)S(1)}, f32[1,512]{1,0:T(1,128)}, u32[]{:S(2)}) copy-start(f32[1,512]{1,0:T(1,128)} %get-tuple-element.252) | copy-start | bytes 6148
  588.3 13.6 %copy-start.51 = (f32[1,512]{1,0:T(1,128)S(1)}, f32[1,512]{1,0:T(1,128)}, u32[]{:S(2)}) copy-start(f32[1,512]{1,0:T(1,128)} %get-tuple-element.251) | copy-start | bytes 6148
  588.3 13.7 %copy-start.60 = (f32[1,512]{1,0:T(1,128)S(1)}, f32[1,512]{1,0:T(1,128)}, u32[]{:S(2)}) copy-start(f32[1,512]{1,0:T(1,128)} %get-tuple-element.259) | copy-start | bytes 6148
  588.4 13.7 %copy-start.61 = (f32[1,512]{1,0:T(1,128)S(1)}, f32[1,512]{1,0:T(1,128)}, u32[]{:S(2)}) copy-start(f32[1,512]{1,0:T(1,128)} %get-tuple-element.260) | copy-start | bytes 6148
  588.4 13.7 %copy-start.62 = (f32[1,512]{1,0:T(1,128)S(1)}, f32[1,512]{1,0:T(1,128)}, u32[]{:S(2)}) copy-start(f32[1,512]{1,0:T(1,128)} %get-tuple-element.261) | copy-start | bytes 6148
  588.4 13.7 %copy-start.63 = (f32[1,512]{1,0:T(1,128)S(1)}, f32[1,512]{1,0:T(1,128)}, u32[]{:S(2)}) copy-start(f32[1,512]{1,0:T(1,128)} %get-tuple-element.262) | copy-start | bytes 6148
  588.4 15.2 %copy-start.49 = (f32[1,512]{1,0:T(1,128)S(1)}, f32[1,512]{1,0:T(1,128)}, u32[]{:S(2)}) copy-start(f32[1,512]{1,0:T(1,128)} %get-tuple-element.258) | copy-start | bytes 6148
  588.4 15.2 %copy-start.50 = (f32[1,512]{1,0:T(1,128)S(1)}, f32[1,512]{1,0:T(1,128)}, u32[]{:S(2)}) copy-start(f32[1,512]{1,0:T(1,128)} %get-tuple-element.263) | copy-start | bytes 6148
  588.4 16.8 %copy-start.83 = (f32[512]{0:T(512)S(1)}, f32[512]{0:T(512)}, u32[]{:S(2)}) copy-start(f32[512]{0:T(512)} %get-tuple-element.250) | copy-start | bytes 6148
  603.5 10.5 %copy-start.52 = (f32[512]{0:T(512)}, f32[512]{0:T(512)S(1)}, u32[]{:S(2)}) copy-start(f32[512]{0:T(512)S(1)} %get-tuple-element.78) | copy-start | bytes 6148
  603.5 10.5 %copy-start.54 = (f32[512]{0:T(512)}, f32[512]{0:T(512)S(1)}, u32[]{:S(2)}) copy-start(f32[512]{0:T(512)S(1)} %get-tuple-element.79) | copy-start | bytes 6148
  604.6 9.4 copy-start.58
  747.5 13.4 %copy-start.18 = (bf16[12,20,1024]{2,1,0:T(8,128)(2,1)S(1)}, bf16[12,20,1024]{2,1,0:T(8,128)(2,1)}, u32[]{:S(2)}) copy-start(bf16[12,20,1024]{2,1,0:T(8,128)(2,1)} %get-tuple-element.170) | copy-start | bytes 1474564
  774.1 20.5 %copy-start.6 = (bf16[3,128,512]{2,1,0:T(8,128)(2,1)S(1)}, bf16[3,128,512]{2,1,0:T(8,128)(2,1)}, u32[]{:S(2)}) copy-start(bf16[3,128,512]{2,1,0:T(8,128)(2,1)} %copy-done.5) | copy-start | bytes 1179652
  774.1 20.5 %copy-start.21 = (bf16[3,77,4096]{2,1,0:T(8,128)(2,1)S(1)}, bf16[3,77,4096]{2,1,0:T(8,128)(2,1)}, u32[]{:S(2)}) copy-start(bf16[3,77,4096]{2,1,0:T(8,128)(2,1)} %param.26) | copy-start | bytes 5677060
  1038.5 13.2 %copy-start.87 = (f32[64]{0:T(128)}, f32[64]{0:T(128)S(1)}, u32[]{:S(2)}) copy-start(f32[64]{0:T(128)S(1)} %get-tuple-element.350) | copy-start | bytes 772
  (59 other events, 269.6 us)
